TPU v7x, 512 devices: a whole 4x8x8 slice. The times are simulated.
512 devices in a mesh: term: 8 (over y), tensor: 64 (over z, x, core).
Axes of the slice: x: 4, y: 8, z: 8, core: 2. Of those that a mesh axis runs over, the one named last changes fastest.
Arguments:
- theta: bfloat16 [4096, 128, 128], P('tensor'), may hold values from -6 to 6
- left_env: bfloat16 [16, 256, 128, 128], P('term', 'tensor'), may hold values from -0.5 to 0.5
- right_env: bfloat16 [16, 192, 128, 128], P('term', 'tensor'), may hold values from -0.5 to 0.5
- coeff: float32 [16, 16], P('term'), may hold values from -1.8 to 1.8
- left_dims: int32 [256], P('tensor'), may hold values from 16 to 128, as said below
- right_dims: int32 [192], P('tensor'), may hold values from 16 to 128, as said below
- dest_dev: int32 [4096, 1], P('tensor'), may hold values from 0 to 63; in each aligned block of 64 rows (0 to 63, 64 to 127, ...) at most 2 rows name the same one
- right_local: int32 [4096], P('tensor'), may hold values from 0 to 2
Outputs:
- sigma: bfloat16 [4096, 128, 128], P('tensor')
Inputs may be any that keep to these rules, and one draw needn't show every extreme that they name: `left_dims`: some sector has all 128 states. `right_dims`: some sector has all 128 states. `dest_dev`: at most 2 of the 64 blocks of one device name the same device.
All inputs are finite; a program needn't handle non-finite values.
Results may differ from a plain program's by a relative error of at most 0.017.
Values may be sent and summed in bfloat16 or wider, within the bound.
No kernel may reach another device: no remote copies, remote signals or barrier semaphores. Data moves between devices by JAX's collectives and lax.ppermute only.
A program may use at most 128 MiB of HBM per device.

v0:
```python
import jax
import jax.numpy as jnp
from jax import lax
from jax.sharding import PartitionSpec as P

PHYS = 16


def right_side(carried_slots, sector, live_flag, envs, env_dims, state_ids):
    choose = sector[:, None] == jnp.arange(envs.shape[1], dtype=jnp.int32)[None, :]
    live_cols = jnp.sum(jnp.where(choose, env_dims[None, :], 0), axis=1)
    col_keep = (state_ids[None, :] < live_cols[:, None]) & live_flag[:, None]
    masked = jnp.where(
        col_keep[:, None, None, :], carried_slots, jnp.zeros((), carried_slots.dtype)
    )
    picked = jnp.take(envs, sector, axis=1)
    result = jnp.einsum("stij,tskj->sik", masked, picked, preferred_element_type=jnp.float32)
    return jnp.where(col_keep[:, None, :], result, 0.0).astype(jnp.bfloat16)


def on_device(theta, left_env, right_env, coeff, left_dims, right_dims, dest_dev, right_local):
    tensor_count = lax.axis_size("tensor")
    blocks = theta.shape[0]
    states = theta.shape[1]
    sectors_here = left_env.shape[1]
    terms_here = left_env.shape[0]
    capacity = max(2, 2 * blocks // tensor_count)
    block_ids = jnp.arange(blocks, dtype=jnp.int32)
    sector_ids = block_ids // PHYS
    state_ids = jnp.arange(states, dtype=jnp.int32)
    owner_table = sector_ids[:, None] == jnp.arange(sectors_here, dtype=jnp.int32)[None, :]
    left_live = jnp.sum(jnp.where(owner_table, left_dims[None, :], 0), axis=1)
    row_keep = state_ids[None, :] < left_live[:, None]
    shaped = jnp.where(row_keep[:, :, None], theta, jnp.zeros((), theta.dtype))
    shaped = shaped.reshape(sectors_here, PHYS, states, states)
    product = jnp.einsum("tsij,spjk->sptik", left_env, shaped, preferred_element_type=jnp.float32)
    weights = coeff.T.reshape(1, PHYS, terms_here, 1, 1)
    carried = (product * weights).astype(jnp.bfloat16).reshape(blocks, terms_here, states, states)
    target = dest_dev[:, 0]
    same = target[:, None] == target[None, :]
    earlier = block_ids[None, :] < block_ids[:, None]
    rank = jnp.sum(same & earlier, axis=1)
    slot = target * capacity + rank
    outbox = (
        jnp.zeros((tensor_count * capacity, terms_here, states, states), jnp.bfloat16)
        .at[slot]
        .set(carried)
    )
    outbox = outbox.reshape(tensor_count, capacity, terms_here, states, states)
    labels = jnp.full((tensor_count * capacity,), -1, jnp.int32).at[slot].set(right_local)
    labels = labels.reshape(tensor_count, capacity)
    arrived = lax.all_to_all(outbox, "tensor", split_axis=0, concat_axis=0, tiled=True)
    names = lax.all_to_all(labels, "tensor", split_axis=0, concat_axis=0, tiled=True)
    count = arrived.shape[1]
    flat_names = names.reshape(-1)
    result = right_side(
        arrived.reshape(-1, terms_here, states, states),
        jnp.maximum(flat_names, 0),
        flat_names >= 0,
        right_env,
        right_dims,
        state_ids,
    )
    answered = lax.all_to_all(
        result.reshape(tensor_count, count, states, states),
        "tensor",
        split_axis=0,
        concat_axis=0,
        tiled=True,
    )
    partial_value = answered.reshape(tensor_count * capacity, states, states)[slot]
    total = lax.psum(partial_value.astype(jnp.float32).astype(jnp.bfloat16), "term").astype(
        jnp.float32
    )
    return jnp.where(row_keep[:, :, None], total, 0.0).astype(jnp.bfloat16)


def solution(mesh):
    in_specs = (
        P("tensor", None, None),
        P("term", "tensor", None, None),
        P("term", "tensor", None, None),
        P("term", None),
        P("tensor"),
        P("tensor"),
        P("tensor", None),
        P("tensor"),
    )
    out_specs = P("tensor", None, None)
    return jax.shard_map(
        on_device, mesh=mesh, in_specs=in_specs, out_specs=out_specs, check_vma=False
    )
```

profile of v0, /device:TPU:6, one launch (start us, length us, event | category | flops | bytes accessed | tf_op | source)
XLA Modules:
  0.0 471.7 jit_solution(9681276580582095603)
XLA Ops:
  6.5 0.9 convert_reduce_fusion
  7.4 0.7 fusion.11
  8.1 0.9 scatter_custom_fusion
  9.0 0.8 all_to_all.12
  9.8 13.8 %all-to-all-start = ((s32[64,1,2]{2,1,0:T(1,128)}), s32[64,1,2]{2,1,0:T(1,128)S(1)}, u32[]{:S(2)}, u32[]{:S(2)}) async-start(s32[64,1,2]{2,1,0:T(1,128)} %bitcast.3), calls=%async_computation | async-start | bytes 65536 | tf_op jit(solution)/shard_map/all_to_all | solution.py:53
  23.6 0.7 select_reduce_fusion.1
  24.4 0.8 copy.25
  25.2 3.2 broadcast_select_fusion
  28.4 3.6 multiply_convert_fusion
  32.0 6.4 %copy.26 = bf16[64,2,128,128]{3,2,1,0:T(8,128)(2,1)} copy(bf16[64,2,128,128]{2,3,1,0:T(8,128)(2,1)} %bitcast.39) | data formatting | bytes 8388608 | tf_op jit(solution)/shard_map/reshape | solution.py:38
  38.3 5.3 %broadcast_in_dim.112 = bf16[128,2,128,128]{3,2,1,0:T(8,128)(2,1)} broadcast(bf16[]{:T(256)} %constant.43.clone.1), dimensions={} | broadcast | bytes 8388610 | tf_op jit(solution)/shard_map/broadcast_in_dim | solution.py:45
  43.7 12.0 %scatter_fusion = bf16[128,2,128,128]{3,2,1,0:T(8,128)(2,1)} fusion(bf16[128,2,128,128]{3,2,1,0:T(8,128)(2,1)} %broadcast_in_dim.112, s32[64]{0:T(128)S(1)} %fusion.11, bf16[64,2,128,128]{3,2,1,0:T(8,128)(2,1)} %copy.26), kind=kCustom, calls=%fused_computation.3 | custom fusion | bytes 12583168 | tf_op jit(solution)/shard_map/scatter | solution.py:47
  55.6 10.7 %all-to-all-start.1 = ((bf16[64,2,2,128,128]{4,3,2,1,0:T(8,128)(2,1)}), bf16[64,2,2,128,128]{4,3,2,1,0:T(8,128)(2,1)}, u32[]{:S(2)}, u32[]{:S(2)}) async-start(bf16[64,2,2,128,128]{4,3,2,1,0:T(8,128)(2,1)} %bitcast.38), calls=%async_computation.1 | async-start | bytes 16777216 | tf_op jit(solution)/shard_map/all_to_all | solution.py:52
  66.4 0.1 max.21
  66.7 0.1 ge.18
  66.9 6.3 %gather_fusion = bf16[128,2,128,128]{3,2,1,0:T(8,128)(2,1)} fusion(bf16[2,3,128,128]{3,2,1,0:T(8,128)(2,1)S(1)} %copy-done.1, s32[1024]{0:T(1024)S(1)} %pad_clamp_fusion.1), kind=kCustom, calls=%fused_computation | custom fusion | bytes 16777728 | tf_op jit(solution)/shard_map/jit(_take)/gather | solution.py:16
  73.4 176.1 %all-to-all-done.1 = bf16[64,2,2,128,128]{4,3,2,1,0:T(8,128)(2,1)} async-done(((bf16[64,2,2,128,128]{4,3,2,1,0:T(8,128)(2,1)}), bf16[64,2,2,128,128]{4,3,2,1,0:T(8,128)(2,1)}, u32[]{:S(2)}, u32[]{:S(2)}) %all-to-all-start.1) | async-done | bytes 8388640 | tf_op jit(solution)/shard_map/all_to_all | solution.py:52
  249.5 7.2 %bitcast_select_fusion.1 = bf16[128,2,128,128]{3,2,1,0:T(8,128)(2,1)} fusion(bf16[64,2,2,128,128]{4,3,2,1,0:T(8,128)(2,1)} %all-to-all-done.1, pred[128,128]{1,0:T(8,128)(4,1)S(1)} %fusion.9), kind=kLoop, calls=%fused_computation.8 | loop fusion | flops 4194304 | bytes 16793600 | tf_op jit(solution)/shard_map/jit(_where)/select_n | solution.py:13
  256.7 10.2 %fusion = bf16[128,128,128]{2,1,0:T(8,128)(2,1)} fusion(pred[128,128]{1,0:T(8,128)(4,1)S(1)} %fusion.9, bf16[128,2,128,128]{3,2,1,0:T(8,128)(2,1)} %bitcast_select_fusion.1, bf16[128,2,128,128]{3,2,1,0:T(8,128)(2,1)} %gather_fusion, pred[128]{0:T(512)(128)(4,1)S(1)} %broadcast_compare_fusion), kind=kOutput, calls=%fused_computation.5 | convolution fusion | flops 1082130432 | bytes 20988032 | tf_op jit(solution)/shard_map/stij,tskj->sik/dot_general | solution.py:17
  266.9 9.5 %all-to-all-start.2 = ((bf16[64,2,128,128]{3,2,1,0:T(8,128)(2,1)}), bf16[64,2,128,128]{3,2,1,0:T(8,128)(2,1)}, u32[]{:S(2)}, u32[]{:S(2)}) async-start(bf16[64,2,128,128]{3,2,1,0:T(8,128)(2,1)} %bitcast.41), calls=%async_computation.2 | async-start | bytes 8388608 | tf_op jit(solution)/shard_map/all_to_all | solution.py:64
  276.4 96.1 %all-to-all-done.2 = bf16[64,2,128,128]{3,2,1,0:T(8,128)(2,1)} async-done(((bf16[64,2,128,128]{3,2,1,0:T(8,128)(2,1)}), bf16[64,2,128,128]{3,2,1,0:T(8,128)(2,1)}, u32[]{:S(2)}, u32[]{:S(2)}) %all-to-all-start.2) | async-done | bytes 4194336 | tf_op jit(solution)/shard_map/all_to_all | solution.py:64
  372.5 4.3 gather_fusion.1
  376.8 83.6 %all-reduce.2.cloned.1.call-done = bf16[64,128,128]{2,1,0:T(8,128)(2,1)} async-done(((bf16[64,128,128]{2,1,0:T(8,128)(2,1)}), bf16[64,128,128]{2,1,0:T(8,128)(2,1)}) %all-reduce.2.cloned.1.call-update) | async-done | bytes 2097168 | tf_op jit(solution)/shard_map/psum | solution.py:72
  460.5 4.4 select_convert_fusion
  (18 shorter events, 0.6 us)
Async XLA Ops:
  6.5 21.8 %copy-start = (bf16[2,4,128,128]{3,2,1,0:T(8,128)(2,1)S(1)}, bf16[2,4,128,128]{3,2,1,0:T(8,128)(2,1)}, u32[]{:S(2)}) copy-start(bf16[2,4,128,128]{3,2,1,0:T(8,128)(2,1)} %param.9) | copy-start | bytes 786436
  9.8 45.9 %all-to-all-start = ((s32[64,1,2]{2,1,0:T(1,128)}), s32[64,1,2]{2,1,0:T(1,128)S(1)}, u32[]{:S(2)}, u32[]{:S(2)}) async-start(s32[64,1,2]{2,1,0:T(1,128)} %bitcast.3), calls=%async_computation | async-start | bytes 65536 | tf_op jit(solution)/shard_map/all_to_all | solution.py:53
  55.6 11.2 %copy-start.1 = (bf16[2,3,128,128]{3,2,1,0:T(8,128)(2,1)S(1)}, bf16[2,3,128,128]{3,2,1,0:T(8,128)(2,1)}, u32[]{:S(2)}) copy-start(bf16[2,3,128,128]{3,2,1,0:T(8,128)(2,1)} %param.10) | copy-start | bytes 589828
  55.6 193.8 %all-to-all-start.1 = ((bf16[64,2,2,128,128]{4,3,2,1,0:T(8,128)(2,1)}), bf16[64,2,2,128,128]{4,3,2,1,0:T(8,128)(2,1)}, u32[]{:S(2)}, u32[]{:S(2)}) async-start(bf16[64,2,2,128,128]{4,3,2,1,0:T(8,128)(2,1)} %bitcast.38), calls=%async_computation.1 | async-start | bytes 16777216 | tf_op jit(solution)/shard_map/all_to_all | solution.py:52
  66.8 6.3 %copy-start.2 = (s32[3]{0:T(128)S(1)}, s32[3]{0:T(128)}, u32[]{:S(2)}) copy-start(s32[3]{0:T(128)} %param.13) | copy-start | bytes 40
  266.9 105.6 %all-to-all-start.2 = ((bf16[64,2,128,128]{3,2,1,0:T(8,128)(2,1)}), bf16[64,2,128,128]{3,2,1,0:T(8,128)(2,1)}, u32[]{:S(2)}, u32[]{:S(2)}) async-start(bf16[64,2,128,128]{3,2,1,0:T(8,128)(2,1)} %bitcast.41), calls=%async_computation.2 | async-start | bytes 8388608 | tf_op jit(solution)/shard_map/all_to_all | solution.py:64
  276.3 184.1 %all-reduce.2.cloned.1.call-start = ((), (), s32[]{:S(2)}) async-start(), calls=%async_computation.3 | async-start | bytes 4194304 | tf_op jit(solution)/shard_map/psum | solution.py:72
Sparse Core Ops, SparseCore 0:
  377.0 83.4 all-reduce.1
where the time goes:
time: 473 us; the launch traced here: 472 us
  waiting for transfers between devices  356 us (75%)
  local copies, waits for them, and re-layouts  37.1 us (8%)
  starting transfers between devices  34 us (7%)
  other arithmetic  17.6 us (4%)
  matrix products  13.8 us (3%)
  between operations  13.5 us (3%)
    all_to_all x1, waiting for transfers between devices, on_device(): lax.all_to_all(outbox, 'tensor', split_axis=0, concat_axis=0, tiled=True)  176 us
    all_to_all x1, waiting for transfers between devices, on_device(): lax.all_to_all(result.reshape(tensor_count, count, states, states), 'tens...  96.1 us
    psum x1, waiting for transfers between devices, on_device(): lax.psum(partial_value.astype(jnp.float32).astype(jnp.bfloat16), 'term')  83.6 us
    all_to_all x1, starting transfers between devices, on_device(): lax.all_to_all(labels, 'tensor', split_axis=0, concat_axis=0, tiled=True)  13.8 us
    scatter x1, local copies, waits for them, and re-layouts, on_device(): outbox = jnp.zeros((tensor_count * capacity, terms_here, states, states),...  12 us
    all_to_all x1, starting transfers between devices, on_device(): lax.all_to_all(outbox, 'tensor', split_axis=0, concat_axis=0, tiled=True)  10.7 us
    dot_general x1, matrix products, right_side(): jnp.einsum('stij,tskj->sik', masked, picked, preferred_element_type=jnp.f...  10.2 us
    all_to_all x1, starting transfers between devices, on_device(): lax.all_to_all(result.reshape(tensor_count, count, states, states), 'tens...  9.46 us
  transfers between devices with their start and end apart: 4, of which 3 were waited for; matrix products, arithmetic and copies ran while one was open for 8% of the time, Pallas kernels for 0%

commit v1 on v0

v1 whole, which is shorter than its diff:
```python
import jax
import jax.numpy as jnp
from jax import lax
from jax.experimental import pallas as pl
from jax.experimental.pallas import tpu as pltpu
from jax.sharding import Mesh, PartitionSpec as P

PHYS = 16
NT = (((1,), (1,)), ((), ()))
BF = jnp.bfloat16
F32 = jnp.float32


def shift(x, axis, by):
    count = lax.axis_size(axis)
    return lax.ppermute(x, axis, [(i, (i + by) % count) for i in range(count)])


def spread(x, axis, by):
    count = lax.axis_size(axis)
    pairs = []
    for i in range(count):
        pairs += [(2 * i, (i + by) % count * 2), (2 * i + 1, (i - by) % count * 2 + 1)]
    return lax.ppermute(x, (axis, "c"), pairs)


def both_ways(x, axis):
    up = down = x
    pieces, owners = [x], [0]
    for step in range(1, 4):
        up, down = shift(up, axis, 1), shift(down, axis, -1)
        pieces += [up, down]
        owners += [-step, step]
    return pieces + [shift(up, axis, 1)], owners + [-4]


def swap(x):
    return lax.ppermute(x, "c", [(0, 1), (1, 0)])


def contract_kernel(zi_ref, xc_ref, s_ref, c_ref, dims_ref, place_ref, th_own, th_sib, *rest):
    th_refs = (th_own, th_sib)
    l_refs, right = rest[:8], rest[8]
    out_ref, r_ref, th_ref, l_ref, a_ref, sems = rest[9:]
    copies = []

    def fetch(src, dst):
        copy = pltpu.make_async_copy(src, dst, sems.at[len(copies)])
        copy.start()
        copies.append(copy)

    for z in range(8):
        fetch(right.at[z], r_ref.at[z])
    for s in range(4):
        fetch(th_own.at[pl.ds(16 * s, 16)], th_ref.at[0, pl.ds(16 * s, 16)])
    for d, ref in enumerate(l_refs):
        for half in range(2):
            fetch(
                ref.at[half if d < 5 else 1 - half, pl.ds(0, 1024)], l_ref.at[half, place_ref[d]]
            )
    for s in range(4):
        fetch(th_sib.at[pl.ds(16 * s, 16)], th_ref.at[1, pl.ds(16 * s, 16)])
    for copy in copies[:8]:
        copy.wait()

    lane = lax.broadcasted_iota(jnp.int32, (128, 128), 1)
    for half in range(2):
        th, le = th_ref.at[half], l_ref.at[half]

        @pl.loop(0, 4)
        def sector(s):
            pltpu.make_async_copy(
                th_refs[half].at[pl.ds(16 * s, 16)],
                th_ref.at[half, pl.ds(16 * s, 16)],
                sems.at[(8, 28)[half] + s],
            ).wait()
            for pp in range(PHYS // 2):
                prods = []
                for e in range(2):
                    n = s * PHYS + 2 * pp + e
                    row = pl.multiple_of(s_ref[half, n] * 16, 16)
                    tile = r_ref[zi_ref[half, n], :, xc_ref[half, n], pl.ds(row, 16)]
                    prods.append(
                        lax.dot_general(
                            tile.reshape(128, 128), th[n], NT, preferred_element_type=F32
                        )
                    )
                for t in range(16):
                    pair = [
                        prods[e][t * 8 : t * 8 + 8] * c_ref[t, 2 * pp + e] for e in range(2)
                    ]
                    a_ref[pp * 16 : pp * 16 + 16, t * 128 : t * 128 + 128] = jnp.concatenate(
                        pair, axis=0
                    ).astype(BF)
            if half == 0:
                @pl.when(s == 0)
                def left_is_here():
                    for copy in copies[12:28]:
                        copy.wait()

            keep = lane < dims_ref[half, s]
            total = jnp.zeros((128, 128), F32)
            for y in range(8):
                tiles = [
                    jnp.where(
                        keep,
                        le[y, pl.ds(pl.multiple_of((t * 4 + s) * 128, 128), 128), :],
                        jnp.zeros((), BF),
                    )
                    for t in range(2)
                ]
                total += lax.dot_general(
                    a_ref[:, y * 256 : y * 256 + 256],
                    jnp.concatenate(tiles, axis=1),
                    NT,
                    preferred_element_type=F32,
                )
            out_ref[half, pl.ds(pl.multiple_of(s * 128, 128), 128), :] = jnp.where(
                keep, total, 0.0
            ).astype(BF)


def finish_kernel(place_ref, *refs):
    pieces, out_ref, rows_ref = refs[:8], refs[8], refs[9]
    eye = (
        lax.broadcasted_iota(jnp.int32, (128, 128), 0)
        == lax.broadcasted_iota(jnp.int32, (128, 128), 1)
    ).astype(F32).astype(BF)
    for d in range(8):
        row = pl.multiple_of(place_ref[d] * 16, 16)
        rows_ref[:, pl.ds(row, 16), :] = pieces[d][...]
    for n in range(out_ref.shape[0]):
        out_ref[n] = lax.dot_general(eye, rows_ref[n], NT, preferred_element_type=F32).astype(BF)


def on_device(theta, left_env, right_env, coeff, left_dims, right_dims, dest_dev, right_local):
    states = jnp.arange(128, dtype=jnp.int32)
    at_y, core = lax.axis_index("y"), lax.axis_index("c")
    first = core == 0
    toward = 2 * core - 1
    steps = [0] + [toward * k for k in (1, 2, 3, 4)] + [-toward * k for k in (1, 2, 3)]
    place = jnp.stack(
        [(at_y + d + 8) % 8 for d in steps]
    ).astype(jnp.int32)

    right_keep = states[None, :] < right_dims[:, None]
    right = jnp.where(
        right_keep[None, :, :, None] & right_keep[None, :, None, :], right_env, jnp.zeros((), BF)
    )
    right = right.reshape(2, 3, 8, 2, 8, 128).transpose(2, 3, 1, 0, 4, 5).reshape(8, 1, 2, 48, 128)
    block = dest_dev[:, 0] * 3 + right_local
    rows = []
    rest = coeff.reshape(1, 32)
    for _ in range(3):
        head = lax.reduce_precision(rest, 8, 7)
        rows.append(jnp.pad(head, ((0, 0), (0, 96))))
        rest = rest - head
    rows.append(jnp.pad(block.astype(F32)[None, :], ((0, 0), (0, 64))))
    rows.append(jnp.pad(left_dims.astype(F32)[None, :], ((0, 11), (0, 124))))
    extra = jnp.concatenate(rows, axis=0).astype(BF)
    left = jnp.concatenate([left_env.reshape(1024, 128), extra], axis=0)
    right = jnp.broadcast_to(right, (8, 4, 2, 48, 128)).reshape(64, 48, 128)
    right = lax.all_to_all(right, ("y", "x", "c"), split_axis=0, concat_axis=0, tiled=True)
    left, right = lax.optimization_barrier((left, right))
    right = lax.all_gather(right.reshape(8, 8, 48, 128), "z")
    pair = jnp.stack([left, swap(left)])
    theta_sib = swap(theta)
    lefts = [pair] + [spread(pair, "y", k) for k in range(1, 5)]
    lefts += [swap(piece) for piece in lefts[1:4]]

    weights = jnp.stack(
        [piece[int(d > 4), 1024:1027, :32].astype(F32) for d, piece in enumerate(lefts)]
    )
    weights = (weights[:, 0] + weights[:, 1] + weights[:, 2]).reshape(8, 1, 2, PHYS)
    here = place[:, None] == jnp.arange(8, dtype=jnp.int32)[None, :]
    weights = jnp.sum(jnp.where(here[:, :, None, None], weights, 0.0), axis=0).reshape(16, PHYS)
    blocks = jnp.stack([block, lefts[0][1, 1027, :64].astype(F32).astype(jnp.int32)])
    dims = jnp.stack([left_dims, lefts[0][1, 1028, :4].astype(F32).astype(jnp.int32)])

    vmem = pl.BlockSpec(memory_space=pltpu.VMEM)
    smem = pl.BlockSpec(memory_space=pltpu.SMEM)
    hbm = pl.BlockSpec(memory_space=pl.ANY)
    part = pl.pallas_call(
        contract_kernel,
        out_shape=jax.ShapeDtypeStruct((2, 512, 128), BF),
        in_specs=[smem] * 6 + [hbm] * 11,
        out_specs=vmem,
        scratch_shapes=[
            pltpu.VMEM((8, 8, 8, 48, 128), BF),
            pltpu.VMEM((2, 64, 128, 128), BF),
            pltpu.VMEM((2, 8, 1024, 128), BF),
            pltpu.VMEM((128, 2048), BF),
            pltpu.SemaphoreType.DMA((32,)),
        ],
        compiler_params=pltpu.CompilerParams(vmem_limit_bytes=56 * 2**20),
        cost_estimate=pl.CostEstimate(flops=1 << 30, bytes_accessed=16 << 20, transcendentals=0),
    )(
        blocks // 24,
        blocks // 3 % 8,
        blocks % 3,
        weights,
        dims,
        place,
        theta,
        theta_sib,
        *lefts,
        right,
    )

    mine = part[0].reshape(64, 8, 128)
    other = swap(part[1]).reshape(64, 8, 128)
    piece = jnp.concatenate(
        [jnp.where(first, mine, other), jnp.where(first, other, mine)], axis=1
    )
    pieces, owners = both_ways(piece, "y")
    place = jnp.stack([(at_y + o + 8) % 8 for o in owners]).astype(jnp.int32)
    return pl.pallas_call(
        finish_kernel,
        grid=(4,),
        out_shape=jax.ShapeDtypeStruct((64, 128, 128), BF),
        in_specs=[smem] + [pl.BlockSpec((16, 16, 128), lambda i: (i, 0, 0))] * 8,
        out_specs=pl.BlockSpec((16, 128, 128), lambda i: (i, 0, 0)),
        scratch_shapes=[pltpu.VMEM((16, 128, 128), BF)],
        compiler_params=pltpu.CompilerParams(vmem_limit_bytes=16 * 2**20),
        cost_estimate=pl.CostEstimate(flops=1 << 28, bytes_accessed=4 << 20, transcendentals=0),
    )(place, *pieces)


def solution(mesh):
    grid = Mesh(mesh.devices.reshape(8, 8, 4, 2), ("y", "z", "x", "c"))
    tensor = ("z", "x", "c")
    in_specs = (
        P(tensor, None, None),
        P("y", tensor, None, None),
        P("y", tensor, None, None),
        P("y", None),
        P(tensor),
        P(tensor),
        P(tensor, None),
        P(tensor),
    )
    return jax.shard_map(
        on_device, mesh=grid, in_specs=in_specs, out_specs=P(tensor, None, None), check_vma=False
    )
```

time: 473 us -> 194 us (0.41)
  waiting for transfers between devices: 356 us -> 90.7 us
  local copies, waits for them, and re-layouts: 37.1 us -> 5.29 us
  starting transfers between devices: 34 us -> 61.1 us
  Pallas kernels: 0 us -> 17.4 us
  matrix products: 13.8 us -> 0 us
  other arithmetic: 17.6 us -> 4.3 us
    all_to_all x3 -> x1, waiting for transfers between devices: 272 us -> 22.7 us  [on_device(): lax.all_to_all(right, ('y', 'x', 'c'), split_axis=0, concat_axis=0, tiled...]
    psum x1 -> x0, waiting for transfers between devices: 83.6 us -> none  [on_device(): lax.psum(partial_value.astype(jnp.float32).astype(jnp.bfloat16), 'term')]
    ppermute x0 -> x17, waiting for transfers between devices: none -> 67 us  [the longest x4 44 us: spread(): return lax.ppermute(x, (axis, 'c'), pairs)]
    ppermute x0 -> x17, starting transfers between devices: none -> 50.4 us  [the longest x7 23 us: shift(): return lax.ppermute(x, axis, [(i, (i + by) % count) for i in range(count)])]
    all_to_all x3 -> x1, starting transfers between devices: 33.9 us -> 10.6 us  [on_device(): lax.all_to_all(right, ('y', 'x', 'c'), split_axis=0, concat_axis=0, tiled...]
    pallas_call x0 -> x2, Pallas kernels: none -> 17.4 us  [the longest x1 13.7 us: on_device(): pl.pallas_call(contract_kernel, out_shape=jax.ShapeDtypeStruct((2, 512, 1...]
    dot_general x2 -> x0, matrix products: 13.8 us -> none  [the longest x1 10.2 us: right_side(): jnp.einsum('stij,tskj->sik', masked, picked, preferred_element_type=jnp.f...]
    scatter x2 -> x0, local copies, waits for them, and re-layouts: 12.9 us -> none  [the longest x1 12 us: on_device(): outbox = jnp.zeros((tensor_count * capacity, terms_here, states, states),...]
  transfers between devices with their start and end apart: 4 -> 19, of which waited for: 3 -> 12; matrix products, arithmetic and copies ran while one was open for 8% -> 1% of each run, Pallas kernels for 0% -> 0%
where the time goes in v1:
time: 194 us; the launch traced here: 193 us
  waiting for transfers between devices  90.7 us (47%)
  starting transfers between devices  61.1 us (31%)
  Pallas kernels  17.4 us (9%)
  between operations  14 us (7%)
  local copies, waits for them, and re-layouts  5.29 us (3%)
  other arithmetic  4.3 us (2%)
    ppermute x4, waiting for transfers between devices, spread(): return lax.ppermute(x, (axis, 'c'), pairs)  44 us
    ppermute x7, starting transfers between devices, shift(): return lax.ppermute(x, axis, [(i, (i + by) % count) for i in range(count)])  23 us
    all_to_all x1, waiting for transfers between devices, on_device(): lax.all_to_all(right, ('y', 'x', 'c'), split_axis=0, concat_axis=0, tiled...  22.7 us
    ppermute x7, waiting for transfers between devices, shift(): return lax.ppermute(x, axis, [(i, (i + by) % count) for i in range(count)])  18 us
    ppermute x4, starting transfers between devices, spread(): return lax.ppermute(x, (axis, 'c'), pairs)  15.4 us
    pallas_call x1, Pallas kernels, on_device(): pl.pallas_call(contract_kernel, out_shape=jax.ShapeDtypeStruct((2, 512, 1...  13.7 us
    ppermute x6, starting transfers between devices, swap(): return lax.ppermute(x, 'c', [(0, 1), (1, 0)])  12 us
    all_to_all x1, starting transfers between devices, on_device(): lax.all_to_all(right, ('y', 'x', 'c'), split_axis=0, concat_axis=0, tiled...  10.6 us
  transfers between devices with their start and end apart: 19, of which 12 were waited for; matrix products, arithmetic and copies ran while one was open for 1% of the time, Pallas kernels for 0%

profile of v1, /device:TPU:6, one launch (start us, length us, event | category | flops | bytes accessed | tf_op | source)
XLA Modules:
  0.0 192.7 jit_solution(14194766037877159559)
XLA Ops:
  9.5 10.6 %all-to-all-start = ((bf16[64,48,128]{2,1,0:T(8,128)(2,1)}), bf16[64,48,128]{2,1,0:T(8,128)(2,1)S(1)}, u32[]{:S(2)}, u32[]{:S(2)}) async-start(bf16[64,48,128]{2,1,0:T(8,128)(2,1)} %bitcast.16), calls=%async_computation | async-start | bytes 1572864 | tf_op jit(solution)/shard_map/all_to_all | solution.py:163
  20.6 22.7 %all-to-all-done = bf16[64,48,128]{2,1,0:T(8,128)(2,1)S(1)} async-done(((bf16[64,48,128]{2,1,0:T(8,128)(2,1)}), bf16[64,48,128]{2,1,0:T(8,128)(2,1)S(1)}, u32[]{:S(2)}, u32[]{:S(2)}) %all-to-all-start) | async-done | bytes 786464 | tf_op jit(solution)/shard_map/all_to_all | solution.py:163
  44.2 1.9 collective-permute-start.8
  46.3 2.4 %collective-permute-start = (bf16[1040,128]{1,0:T(8,128)(2,1)S(1)}, bf16[1040,128]{1,0:T(8,128)(2,1)S(1)}, u32[]{:S(2)}, u32[]{:S(2)}) collective-permute-start(bf16[1040,128]{1,0:T(8,128)(2,1)S(1)} %concatenate.9), channel_id=1, source_target_pairs={{0,1},{1,0},{2,3},{3,2},{4,5},{5,4},{6,7},{7,6},{8,9},{9,8},{10,11... | collective-permute-start | bytes 798728 | tf_op jit(solution)/shard_map/ppermute | solution.py:38
  50.7 3.0 %collective-permute-start.3 = (bf16[2,1040,128]{2,1,0:T(8,128)(2,1)S(1)}, bf16[2,1040,128]{2,1,0:T(8,128)(2,1)S(1)}, u32[]{:S(2)}, u32[]{:S(2)}) collective-permute-start(bf16[2,1040,128]{2,1,0:T(8,128)(2,1)S(1)} %pad_maximum_fusion.rest_0_), channel_id=1, source_target_pairs={{0,192},{1,321},{64,256},{65,385},{128,320},{129,449},{192,384},{1... | collective-permute-start | bytes 1597448 | tf_op jit(solution)/shard_map/ppermute | solution.py:24
  53.7 2.9 %collective-permute-start.2 = (bf16[2,1040,128]{2,1,0:T(8,128)(2,1)S(1)}, bf16[2,1040,128]{2,1,0:T(8,128)(2,1)S(1)}, u32[]{:S(2)}, u32[]{:S(2)}) collective-permute-start(bf16[2,1040,128]{2,1,0:T(8,128)(2,1)S(1)} %pad_maximum_fusion.rest_0_), channel_id=1, source_target_pairs={{0,128},{1,385},{64,192},{65,449},{128,256},{129,1},{192,320},{193... | collective-permute-start | bytes 1597448 | tf_op jit(solution)/shard_map/ppermute | solution.py:24
  56.6 3.2 %collective-permute-start.1 = (bf16[2,1040,128]{2,1,0:T(8,128)(2,1)S(1)}, bf16[2,1040,128]{2,1,0:T(8,128)(2,1)S(1)}, u32[]{:S(2)}, u32[]{:S(2)}) collective-permute-start(bf16[2,1040,128]{2,1,0:T(8,128)(2,1)S(1)} %pad_maximum_fusion.rest_0_), channel_id=1, source_target_pairs={{0,64},{1,449},{64,128},{65,1},{128,192},{129,65},{192,256},{193,1... | collective-permute-start | bytes 1597448 | tf_op jit(solution)/shard_map/ppermute | solution.py:24
  59.8 6.3 %collective-permute-start.4 = (bf16[2,1040,128]{2,1,0:T(8,128)(2,1)S(1)}, bf16[2,1040,128]{2,1,0:T(8,128)(2,1)S(1)}, u32[]{:S(2)}, u32[]{:S(2)}) collective-permute-start(bf16[2,1040,128]{2,1,0:T(8,128)(2,1)S(1)} %pad_maximum_fusion.rest_0_), channel_id=1, source_target_pairs={{0,256},{1,257},{64,320},{65,321},{128,384},{129,385},{192,448},{1... | collective-permute-start | bytes 1597448 | tf_op jit(solution)/shard_map/ppermute | solution.py:24
  67.4 12.1 %collective-permute-done.3.rest_3_ = bf16[2,1040,128]{2,1,0:T(8,128)(2,1)S(1)} collective-permute-done((bf16[2,1040,128]{2,1,0:T(8,128)(2,1)S(1)}, bf16[2,1040,128]{2,1,0:T(8,128)(2,1)S(1)}, u32[]{:S(2)}, u32[]{:S(2)}) %collective-permute-start.3) | collective-permute-done | bytes 532512 | tf_op jit(solution)/shard_map/ppermute | solution.py:24
  81.3 15.4 %collective-permute-done.2.rest_2_ = bf16[2,1040,128]{2,1,0:T(8,128)(2,1)S(1)} collective-permute-done((bf16[2,1040,128]{2,1,0:T(8,128)(2,1)S(1)}, bf16[2,1040,128]{2,1,0:T(8,128)(2,1)S(1)}, u32[]{:S(2)}, u32[]{:S(2)}) %collective-permute-start.2) | collective-permute-done | bytes 532512 | tf_op jit(solution)/shard_map/ppermute | solution.py:24
  98.7 16.5 %collective-permute-done.1.rest_1_ = bf16[2,1040,128]{2,1,0:T(8,128)(2,1)S(1)} collective-permute-done((bf16[2,1040,128]{2,1,0:T(8,128)(2,1)S(1)}, bf16[2,1040,128]{2,1,0:T(8,128)(2,1)S(1)}, u32[]{:S(2)}, u32[]{:S(2)}) %collective-permute-start.1) | collective-permute-done | bytes 532512 | tf_op jit(solution)/shard_map/ppermute | solution.py:24
  115.2 1.9 collective-permute-start.5
  122.0 13.7 %shard_map.82 = bf16[2,512,128]{2,1,0:T(8,128)(2,1)} custom-call(s32[2,64]{1,0:T(2,128)} %get-tuple-element.13.zi_ref, s32[2,64]{1,0:T(2,128)} %get-tuple-element.12.xc_ref, s32[2,64]{1,0:T(2,128)} %get-tuple-element.11.s_ref, f32[16,16]{1,0:T(8,128)} %bitcast.62, s32[2,4]{1,0:T(2,128)} %pad_add_fusion.1.dims_ref, s32[8]{0:T(128)} %copy-done.11, ...), custom_call_target="tpu_custom_call" | custom-call | flops 1073741824 | bytes 16777216 | tf_op jit(solution)/shard_map/pallas_call | solution.py:183
  136.6 1.9 collective-permute-start.9
  140.8 3.4 %collective-permute-start.10 = (bf16[64,16,128]{2,1,0:T(8,128)(2,1)S(1)}, bf16[64,16,128]{2,1,0:T(8,128)(2,1)S(1)}, u32[]{:S(2)}, u32[]{:S(2)}) collective-permute-start(bf16[64,16,128]{2,1,0:T(8,128)(2,1)S(1)} %pad_maximum_fusion.1.refs_0_), channel_id=1, source_target_pairs={{0,64},{64,128},{128,192},{192,256},{256,320},{320,384},{384,448},... | collective-permute-start | bytes 786440 | tf_op jit(solution)/shard_map/ppermute | solution.py:16
  144.3 3.7 %collective-permute-start.11 = (bf16[64,16,128]{2,1,0:T(8,128)(2,1)S(1)}, bf16[64,16,128]{2,1,0:T(8,128)(2,1)S(1)}, u32[]{:S(2)}, u32[]{:S(2)}) collective-permute-start(bf16[64,16,128]{2,1,0:T(8,128)(2,1)S(1)} %pad_maximum_fusion.1.refs_0_), channel_id=1, source_target_pairs={{0,448},{64,0},{128,64},{192,128},{256,192},{320,256},{384,320},{4... | collective-permute-start | bytes 786440 | tf_op jit(solution)/shard_map/ppermute | solution.py:16
  147.9 4.4 %collective-permute-done.10.refs_1_ = bf16[64,16,128]{2,1,0:T(8,128)(2,1)S(1)} collective-permute-done((bf16[64,16,128]{2,1,0:T(8,128)(2,1)S(1)}, bf16[64,16,128]{2,1,0:T(8,128)(2,1)S(1)}, u32[]{:S(2)}, u32[]{:S(2)}) %collective-permute-start.10) | collective-permute-done | bytes 262176 | tf_op jit(solution)/shard_map/ppermute | solution.py:16
  152.3 2.2 %collective-permute-start.12 = (bf16[64,16,128]{2,1,0:T(8,128)(2,1)S(1)}, bf16[64,16,128]{2,1,0:T(8,128)(2,1)S(1)}, u32[]{:S(2)}, u32[]{:S(2)}) collective-permute-start(bf16[64,16,128]{2,1,0:T(8,128)(2,1)S(1)} %collective-permute-done.10.refs_1_), channel_id=1, source_target_pairs={{0,64},{64,128},{128,192},{192,256},{256,320},{320,384},{384,448},... | collective-permute-start | bytes 786440 | tf_op jit(solution)/shard_map/ppermute | solution.py:16
  154.5 4.9 %collective-permute-start.13 = (bf16[64,16,128]{2,1,0:T(8,128)(2,1)S(1)}, bf16[64,16,128]{2,1,0:T(8,128)(2,1)S(1)}, u32[]{:S(2)}, u32[]{:S(2)}) collective-permute-start(bf16[64,16,128]{2,1,0:T(8,128)(2,1)S(1)} %collective-permute-done.11.refs_2_), channel_id=1, source_target_pairs={{0,448},{64,0},{128,64},{192,128},{256,192},{320,256},{384,320},{4... | collective-permute-start | bytes 786440 | tf_op jit(solution)/shard_map/ppermute | solution.py:16
  159.4 3.6 %collective-permute-done.12.refs_3_ = bf16[64,16,128]{2,1,0:T(8,128)(2,1)S(1)} collective-permute-done((bf16[64,16,128]{2,1,0:T(8,128)(2,1)S(1)}, bf16[64,16,128]{2,1,0:T(8,128)(2,1)S(1)}, u32[]{:S(2)}, u32[]{:S(2)}) %collective-permute-start.12) | collective-permute-done | bytes 262176 | tf_op jit(solution)/shard_map/ppermute | solution.py:16
  164.9 5.1 %collective-permute-start.15 = (bf16[64,16,128]{2,1,0:T(8,128)(2,1)S(1)}, bf16[64,16,128]{2,1,0:T(8,128)(2,1)S(1)}, u32[]{:S(2)}, u32[]{:S(2)}) collective-permute-start(bf16[64,16,128]{2,1,0:T(8,128)(2,1)S(1)} %collective-permute-done.13.refs_4_), channel_id=1, source_target_pairs={{0,448},{64,0},{128,64},{192,128},{256,192},{320,256},{384,320},{4... | collective-permute-start | bytes 786440 | tf_op jit(solution)/shard_map/ppermute | solution.py:16
  170.0 2.6 %collective-permute-done.14.refs_5_ = bf16[64,16,128]{2,1,0:T(8,128)(2,1)S(1)} collective-permute-done((bf16[64,16,128]{2,1,0:T(8,128)(2,1)S(1)}, bf16[64,16,128]{2,1,0:T(8,128)(2,1)S(1)}, u32[]{:S(2)}, u32[]{:S(2)}) %collective-permute-start.14) | collective-permute-done | bytes 262176 | tf_op jit(solution)/shard_map/ppermute | solution.py:16
  174.7 7.4 %collective-permute-done.16.refs_7_ = bf16[64,16,128]{2,1,0:T(8,128)(2,1)S(1)} collective-permute-done((bf16[64,16,128]{2,1,0:T(8,128)(2,1)S(1)}, bf16[64,16,128]{2,1,0:T(8,128)(2,1)S(1)}, u32[]{:S(2)}, u32[]{:S(2)}) %collective-permute-start.16) | collective-permute-done | bytes 262176 | tf_op jit(solution)/shard_map/ppermute | solution.py:16
  182.1 3.8 %shard_map.83 = bf16[64,128,128]{2,1,0:T(8,128)(2,1)} custom-call(s32[8]{0:T(128)S(1)} %stack.97.place_ref, bf16[64,16,128]{2,1,0:T(8,128)(2,1)S(1)} %pad_maximum_fusion.1.refs_0_, bf16[64,16,128]{2,1,0:T(8,128)(2,1)S(1)} %collective-permute-done.10.refs_1_, bf16[64,16,128]{2,1,0:T(8,128)(2,1)S(1)} %collective-permute-done.11.refs_2_, ...), custom_call_target="tpu_custom_call" | custom-call | flops 268435456 | bytes 4194304 | tf_op jit(solution)/shard_map/pallas_call | solution.py:217
  (88 shorter events, 23.3 us)
Async XLA Ops:
  8.4 35.8 %copy-start.2 = (bf16[64,128,128]{2,1,0:T(8,128)(2,1)S(1)}, bf16[64,128,128]{2,1,0:T(8,128)(2,1)}, u32[]{:S(2)}) copy-start(bf16[64,128,128]{2,1,0:T(8,128)(2,1)} %th_own.1) | copy-start | bytes 6291460
  9.5 33.8 %all-to-all-start = ((bf16[64,48,128]{2,1,0:T(8,128)(2,1)}), bf16[64,48,128]{2,1,0:T(8,128)(2,1)S(1)}, u32[]{:S(2)}, u32[]{:S(2)}) async-start(bf16[64,48,128]{2,1,0:T(8,128)(2,1)} %bitcast.16), calls=%async_computation | async-start | bytes 1572864 | tf_op jit(solution)/shard_map/all_to_all | solution.py:163
  20.1 102.0 %all-gather.2.cloned.1.call-start = ((), (), s32[]{:S(2)}) async-start(), calls=%async_computation.1 | async-start | bytes 7077888 | tf_op jit(solution)/shard_map/all_gather | solution.py:165
  44.2 76.8 %collective-permute-start.8 = (bf16[64,128,128]{2,1,0:T(8,128)(2,1)S(1)}, bf16[64,128,128]{2,1,0:T(8,128)(2,1)}, u32[]{:S(2)}, u32[]{:S(2)}) collective-permute-start(bf16[64,128,128]{2,1,0:T(8,128)(2,1)S(1)} %copy-done.2), channel_id=1, source_target_pairs={{0,1},{1,0},{2,3},{3,2},{4,5},{5,4},{6,7},{7,6},{8,9},{9,8},{10,11... | collective-permute-start | bytes 6291464 | tf_op jit(solution)/shard_map/ppermute | solution.py:38
  46.3 75.7 %copy-start.11 = (s32[8]{0:T(128)}, s32[8]{0:T(128)S(1)}, u32[]{:S(2)}) copy-start(s32[8]{0:T(128)S(1)} %stack.108.place_ref) | copy-start | bytes 100
  46.3 4.3 %collective-permute-start = (bf16[1040,128]{1,0:T(8,128)(2,1)S(1)}, bf16[1040,128]{1,0:T(8,128)(2,1)S(1)}, u32[]{:S(2)}, u32[]{:S(2)}) collective-permute-start(bf16[1040,128]{1,0:T(8,128)(2,1)S(1)} %concatenate.9), channel_id=1, source_target_pairs={{0,1},{1,0},{2,3},{3,2},{4,5},{5,4},{6,7},{7,6},{8,9},{9,8},{10,11... | collective-permute-start | bytes 798728 | tf_op jit(solution)/shard_map/ppermute | solution.py:38
  50.7 71.4 %copy-start.1 = (bf16[2,1040,128]{2,1,0:T(8,128)(2,1)}, bf16[2,1040,128]{2,1,0:T(8,128)(2,1)S(1)}, u32[]{:S(2)}) copy-start(bf16[2,1040,128]{2,1,0:T(8,128)(2,1)S(1)} %pad_maximum_fusion.rest_0_) | copy-start | bytes 1597444
  50.7 28.7 %collective-permute-start.3 = (bf16[2,1040,128]{2,1,0:T(8,128)(2,1)S(1)}, bf16[2,1040,128]{2,1,0:T(8,128)(2,1)S(1)}, u32[]{:S(2)}, u32[]{:S(2)}) collective-permute-start(bf16[2,1040,128]{2,1,0:T(8,128)(2,1)S(1)} %pad_maximum_fusion.rest_0_), channel_id=1, source_target_pairs={{0,192},{1,321},{64,256},{65,385},{128,320},{129,449},{192,384},{1... | collective-permute-start | bytes 1597448 | tf_op jit(solution)/shard_map/ppermute | solution.py:24
  53.7 43.1 %collective-permute-start.2 = (bf16[2,1040,128]{2,1,0:T(8,128)(2,1)S(1)}, bf16[2,1040,128]{2,1,0:T(8,128)(2,1)S(1)}, u32[]{:S(2)}, u32[]{:S(2)}) collective-permute-start(bf16[2,1040,128]{2,1,0:T(8,128)(2,1)S(1)} %pad_maximum_fusion.rest_0_), channel_id=1, source_target_pairs={{0,128},{1,385},{64,192},{65,449},{128,256},{129,1},{192,320},{193... | collective-permute-start | bytes 1597448 | tf_op jit(solution)/shard_map/ppermute | solution.py:24
  56.6 58.6 %collective-permute-start.1 = (bf16[2,1040,128]{2,1,0:T(8,128)(2,1)S(1)}, bf16[2,1040,128]{2,1,0:T(8,128)(2,1)S(1)}, u32[]{:S(2)}, u32[]{:S(2)}) collective-permute-start(bf16[2,1040,128]{2,1,0:T(8,128)(2,1)S(1)} %pad_maximum_fusion.rest_0_), channel_id=1, source_target_pairs={{0,64},{1,449},{64,128},{65,1},{128,192},{129,65},{192,256},{193,1... | collective-permute-start | bytes 1597448 | tf_op jit(solution)/shard_map/ppermute | solution.py:24
  59.8 57.3 %collective-permute-start.4 = (bf16[2,1040,128]{2,1,0:T(8,128)(2,1)S(1)}, bf16[2,1040,128]{2,1,0:T(8,128)(2,1)S(1)}, u32[]{:S(2)}, u32[]{:S(2)}) collective-permute-start(bf16[2,1040,128]{2,1,0:T(8,128)(2,1)S(1)} %pad_maximum_fusion.rest_0_), channel_id=1, source_target_pairs={{0,256},{1,257},{64,320},{65,321},{128,384},{129,385},{192,448},{1... | collective-permute-start | bytes 1597448 | tf_op jit(solution)/shard_map/ppermute | solution.py:24
  79.4 42.6 %copy-start.3 = (bf16[2,1040,128]{2,1,0:T(8,128)(2,1)}, bf16[2,1040,128]{2,1,0:T(8,128)(2,1)S(1)}, u32[]{:S(2)}) copy-start(bf16[2,1040,128]{2,1,0:T(8,128)(2,1)S(1)} %collective-permute-done.3.rest_3_) | copy-start | bytes 1597444
  79.4 39.6 %collective-permute-start.7 = (bf16[2,1040,128]{2,1,0:T(8,128)(2,1)S(1)}, bf16[2,1040,128]{2,1,0:T(8,128)(2,1)S(1)}, u32[]{:S(2)}, u32[]{:S(2)}) collective-permute-start(bf16[2,1040,128]{2,1,0:T(8,128)(2,1)S(1)} %collective-permute-done.3.rest_3_), channel_id=1, source_target_pairs={{0,1},{1,0},{2,3},{3,2},{4,5},{5,4},{6,7},{7,6},{8,9},{9,8},{10,11... | collective-permute-start | bytes 1597448 | tf_op jit(solution)/shard_map/ppermute | solution.py:38
  96.7 22.3 %copy-start.4 = (bf16[2,1040,128]{2,1,0:T(8,128)(2,1)}, bf16[2,1040,128]{2,1,0:T(8,128)(2,1)S(1)}, u32[]{:S(2)}) copy-start(bf16[2,1040,128]{2,1,0:T(8,128)(2,1)S(1)} %collective-permute-done.2.rest_2_) | copy-start | bytes 1597444
  96.7 22.2 %collective-permute-start.6 = (bf16[2,1040,128]{2,1,0:T(8,128)(2,1)S(1)}, bf16[2,1040,128]{2,1,0:T(8,128)(2,1)S(1)}, u32[]{:S(2)}, u32[]{:S(2)}) collective-permute-start(bf16[2,1040,128]{2,1,0:T(8,128)(2,1)S(1)} %collective-permute-done.2.rest_2_), channel_id=1, source_target_pairs={{0,1},{1,0},{2,3},{3,2},{4,5},{5,4},{6,7},{7,6},{8,9},{9,8},{10,11... | collective-permute-start | bytes 1597448 | tf_op jit(solution)/shard_map/ppermute | solution.py:38
  115.2 3.8 %collective-permute-start.5 = (bf16[2,1040,128]{2,1,0:T(8,128)(2,1)S(1)}, bf16[2,1040,128]{2,1,0:T(8,128)(2,1)S(1)}, u32[]{:S(2)}, u32[]{:S(2)}) collective-permute-start(bf16[2,1040,128]{2,1,0:T(8,128)(2,1)S(1)} %collective-permute-done.1.rest_1_), channel_id=1, source_target_pairs={{0,1},{1,0},{2,3},{3,2},{4,5},{5,4},{6,7},{7,6},{8,9},{9,8},{10,11... | collective-permute-start | bytes 1597448 | tf_op jit(solution)/shard_map/ppermute | solution.py:38
  136.6 3.2 %collective-permute-start.9 = (bf16[512,128]{1,0:T(8,128)(2,1)S(1)}, bf16[512,128]{1,0:T(8,128)(2,1)S(1)}, u32[]{:S(2)}, u32[]{:S(2)}) collective-permute-start(bf16[512,128]{1,0:T(8,128)(2,1)S(1)} %slice_bitcast_fusion), channel_id=1, source_target_pairs={{0,1},{1,0},{2,3},{3,2},{4,5},{5,4},{6,7},{7,6},{8,9},{9,8},{10,11... | collective-permute-start | bytes 393224 | tf_op jit(solution)/shard_map/ppermute | solution.py:38
  140.8 11.5 %collective-permute-start.10 = (bf16[64,16,128]{2,1,0:T(8,128)(2,1)S(1)}, bf16[64,16,128]{2,1,0:T(8,128)(2,1)S(1)}, u32[]{:S(2)}, u32[]{:S(2)}) collective-permute-start(bf16[64,16,128]{2,1,0:T(8,128)(2,1)S(1)} %pad_maximum_fusion.1.refs_0_), channel_id=1, source_target_pairs={{0,64},{64,128},{128,192},{192,256},{256,320},{320,384},{384,448},... | collective-permute-start | bytes 786440 | tf_op jit(solution)/shard_map/ppermute | solution.py:16
  144.3 10.2 %collective-permute-start.11 = (bf16[64,16,128]{2,1,0:T(8,128)(2,1)S(1)}, bf16[64,16,128]{2,1,0:T(8,128)(2,1)S(1)}, u32[]{:S(2)}, u32[]{:S(2)}) collective-permute-start(bf16[64,16,128]{2,1,0:T(8,128)(2,1)S(1)} %pad_maximum_fusion.1.refs_0_), channel_id=1, source_target_pairs={{0,448},{64,0},{128,64},{192,128},{256,192},{320,256},{384,320},{4... | collective-permute-start | bytes 786440 | tf_op jit(solution)/shard_map/ppermute | solution.py:16
  152.3 10.6 %collective-permute-start.12 = (bf16[64,16,128]{2,1,0:T(8,128)(2,1)S(1)}, bf16[64,16,128]{2,1,0:T(8,128)(2,1)S(1)}, u32[]{:S(2)}, u32[]{:S(2)}) collective-permute-start(bf16[64,16,128]{2,1,0:T(8,128)(2,1)S(1)} %collective-permute-done.10.refs_1_), channel_id=1, source_target_pairs={{0,64},{64,128},{128,192},{192,256},{256,320},{320,384},{384,448},... | collective-permute-start | bytes 786440 | tf_op jit(solution)/shard_map/ppermute | solution.py:16
  154.5 10.3 %collective-permute-start.13 = (bf16[64,16,128]{2,1,0:T(8,128)(2,1)S(1)}, bf16[64,16,128]{2,1,0:T(8,128)(2,1)S(1)}, u32[]{:S(2)}, u32[]{:S(2)}) collective-permute-start(bf16[64,16,128]{2,1,0:T(8,128)(2,1)S(1)} %collective-permute-done.11.refs_2_), channel_id=1, source_target_pairs={{0,448},{64,0},{128,64},{192,128},{256,192},{320,256},{384,320},{4... | collective-permute-start | bytes 786440 | tf_op jit(solution)/shard_map/ppermute | solution.py:16
  162.9 9.7 %collective-permute-start.14 = (bf16[64,16,128]{2,1,0:T(8,128)(2,1)S(1)}, bf16[64,16,128]{2,1,0:T(8,128)(2,1)S(1)}, u32[]{:S(2)}, u32[]{:S(2)}) collective-permute-start(bf16[64,16,128]{2,1,0:T(8,128)(2,1)S(1)} %collective-permute-done.12.refs_3_), channel_id=1, source_target_pairs={{0,64},{64,128},{128,192},{192,256},{256,320},{320,384},{384,448},... | collective-permute-start | bytes 786440 | tf_op jit(solution)/shard_map/ppermute | solution.py:16
  164.9 9.8 %collective-permute-start.15 = (bf16[64,16,128]{2,1,0:T(8,128)(2,1)S(1)}, bf16[64,16,128]{2,1,0:T(8,128)(2,1)S(1)}, u32[]{:S(2)}, u32[]{:S(2)}) collective-permute-start(bf16[64,16,128]{2,1,0:T(8,128)(2,1)S(1)} %collective-permute-done.13.refs_4_), channel_id=1, source_target_pairs={{0,448},{64,0},{128,64},{192,128},{256,192},{320,256},{384,320},{4... | collective-permute-start | bytes 786440 | tf_op jit(solution)/shard_map/ppermute | solution.py:16
  172.6 9.5 %collective-permute-start.16 = (bf16[64,16,128]{2,1,0:T(8,128)(2,1)S(1)}, bf16[64,16,128]{2,1,0:T(8,128)(2,1)S(1)}, u32[]{:S(2)}, u32[]{:S(2)}) collective-permute-start(bf16[64,16,128]{2,1,0:T(8,128)(2,1)S(1)} %collective-permute-done.14.refs_5_), channel_id=1, source_target_pairs={{0,64},{64,128},{128,192},{192,256},{256,320},{320,384},{384,448},... | collective-permute-start | bytes 786440 | tf_op jit(solution)/shard_map/ppermute | solution.py:16
  (11 other events, 78.2 us)
Sparse Core Ops, SparseCore 0:
  44.3 77.6 all-gather.1

commit v2 on v1

v2 whole, which is shorter than its diff:
```python
import jax
import jax.numpy as jnp
from jax import lax
from jax.experimental import pallas as pl
from jax.experimental.pallas import tpu as pltpu
from jax.sharding import Mesh, PartitionSpec as P

PHYS = 16
NT = (((1,), (1,)), ((), ()))
BF = jnp.bfloat16
F32 = jnp.float32


def shift(x, axis, by):
    count = lax.axis_size(axis)
    return lax.ppermute(x, axis, [(i, (i + by) % count) for i in range(count)])


def both_ways(x, axis):
    up = down = x
    pieces, owners = [x], [0]
    for step in range(1, 4):
        up, down = shift(up, axis, 1), shift(down, axis, -1)
        pieces += [up, down]
        owners += [-step, step]
    return pieces + [shift(up, axis, 1)], owners + [-4]


def swap(x):
    return lax.ppermute(x, "c", [(0, 1), (1, 0)])


def flip(rows):
    eye = (
        lax.broadcasted_iota(jnp.int32, (128, 128), 0)
        == lax.broadcasted_iota(jnp.int32, (128, 128), 1)
    ).astype(F32).astype(BF)
    return lax.dot_general(eye, rows, NT, preferred_element_type=F32).astype(BF)


def theta_kernel(th_own, th_sib, out_ref):
    for half, th in enumerate((th_own, th_sib)):
        @pl.loop(0, 8)
        def some(i):
            for k in range(8):
                out_ref[half, i * 8 + k] = flip(th[i * 8 + k])


def left_kernel(l_own, l_sib, out_ref, sems):
    copies = [
        pltpu.make_async_copy(ref.at[y], out_ref.at[half, y], sems.at[half, y])
        for half, ref in enumerate((l_own, l_sib))
        for y in range(8)
    ]
    for copy in copies:
        copy.start()
    for copy in copies:
        copy.wait()


def contract_kernel(zi_ref, xc_ref, s_ref, c_ref, dims_ref, place_ref, th_ref, l_ref, *rest):
    two, one = rest[0], rest[1:6]
    out_refs, (r_ref, a_ref, sems) = rest[6:8], rest[8:]
    copies = []

    def fetch(src, dst):
        copy = pltpu.make_async_copy(src, dst, sems.at[len(copies)])
        copy.start()
        copies.append(copy)

    for z in range(8):
        fetch(two.at[z], r_ref.at[z, :, :, :, pl.ds(0, 32)])
    for d in range(3):
        fetch(one[d], r_ref.at[:, place_ref[d], :, :, pl.ds(32, 16)])
    for d in range(2):
        fetch(one[3 + d], r_ref.at[pl.ds(4 * d, 4), place_ref[3], :, :, pl.ds(32, 16)])
    for copy in copies:
        copy.wait()

    lane = lax.broadcasted_iota(jnp.int32, (128, 128), 1)
    for half in range(2):
        @pl.loop(0, 4, unroll=4)
        def sector(s):
            for pp in range(PHYS // 2):
                prods = []
                for e in range(2):
                    n = s * PHYS + 2 * pp + e
                    row = pl.multiple_of(s_ref[half, n] * 16, 16)
                    xc = xc_ref[half, n]
                    tile = r_ref[zi_ref[half, n], xc // 2, :, xc % 2, pl.ds(row, 16)]
                    prods.append(
                        jnp.dot(
                            tile.reshape(128, 128), th_ref[half, n], preferred_element_type=F32
                        )
                    )
                for t in range(16):
                    pair = [
                        prods[e][t * 8 : t * 8 + 8] * c_ref[t, 2 * pp + e] for e in range(2)
                    ]
                    a_ref[s, pp * 16 : pp * 16 + 16, t * 128 : t * 128 + 128] = jnp.concatenate(
                        pair, axis=0
                    ).astype(BF)
            keep = lane < dims_ref[half, s]
            total = jnp.zeros((128, 128), F32)
            for y in range(8):
                tiles = [
                    jnp.where(keep, l_ref[half, y, t, s], jnp.zeros((), BF)) for t in range(2)
                ]
                total += lax.dot_general(
                    a_ref[s, :, y * 256 : y * 256 + 256],
                    jnp.concatenate(tiles, axis=1),
                    NT,
                    preferred_element_type=F32,
                )
            out_refs[half][pl.ds(pl.multiple_of(s * 128, 128), 128), :] = jnp.where(
                keep, total, 0.0
            ).astype(BF)


def finish_kernel(place_ref, *refs):
    pieces, out_ref, rows_ref = refs[:8], refs[8], refs[9]
    for d in range(8):
        row = pl.multiple_of(place_ref[d] * 16, 16)
        rows_ref[:, pl.ds(row, 16), :] = pieces[d][...]
    for n in range(out_ref.shape[0]):
        out_ref[n] = flip(rows_ref[n])


def on_device(theta, left_env, right_env, coeff, left_dims, right_dims, dest_dev, right_local):
    states = jnp.arange(128, dtype=jnp.int32)
    at_y, at_x = lax.axis_index("y"), lax.axis_index("x")
    first = lax.axis_index("c") == 0

    right_keep = states[None, :] < right_dims[:, None]
    right = jnp.where(
        right_keep[None, :, :, None] & right_keep[None, :, None, :], right_env, jnp.zeros((), BF)
    )
    right = right.reshape(2, 3, 8, 2, 8, 128).transpose(2, 3, 1, 0, 4, 5).reshape(8, 1, 2, 48, 128)
    block = dest_dev[:, 0] * 3 + right_local
    facts = jnp.stack([block, jnp.pad(left_dims, (0, 60))])
    facts = jnp.stack([facts, swap(facts)])
    blocks, dims = facts[:, 0], facts[:, 1, :4]
    parts = []
    rest = coeff.reshape(1, 32)
    for _ in range(3):
        head = lax.reduce_precision(rest, 8, 7)
        parts.append(head.astype(BF))
        rest = rest - head
    extra = jnp.pad(jnp.concatenate(parts, axis=0), ((0, 13), (0, 96)))
    right = jnp.concatenate(
        [right.reshape(16, 48, 128), jnp.broadcast_to(extra[None], (16, 16, 128))], axis=1
    )
    left_own = lax.all_gather(left_env, "y")
    right = lax.all_to_all(
        right, ("y", "c"), split_axis=0, concat_axis=0, tiled=True
    ).reshape(8, 2, 64, 128)
    two = jnp.broadcast_to(right[None, :, :, :32], (4, 8, 2, 32, 128))
    two = lax.all_to_all(two, "x", split_axis=0, concat_axis=0, tiled=True)
    one, two = lax.optimization_barrier((right[:, :, 32:48], two))
    two = lax.all_gather(two, "z")
    one = jnp.broadcast_to(one[None], (8, 8, 2, 16, 128))
    one = lax.all_to_all(one, "z", split_axis=0, concat_axis=0, tiled=True)
    theta_sib = swap(theta)
    weights = right[:, 0, 48:51, :32].astype(F32)
    weights = (weights[:, 0] + weights[:, 1] + weights[:, 2]).reshape(16, PHYS)
    vmem = pl.BlockSpec(memory_space=pltpu.VMEM)
    smem = pl.BlockSpec(memory_space=pltpu.SMEM)
    hbm = pl.BlockSpec(memory_space=pl.ANY)

    def settings(mib, flops, traffic):
        return dict(
            compiler_params=pltpu.CompilerParams(vmem_limit_bytes=mib * 2**20),
            cost_estimate=pl.CostEstimate(
                flops=flops, bytes_accessed=traffic << 20, transcendentals=0
            ),
        )

    flipped = pl.pallas_call(
        theta_kernel,
        out_shape=jax.ShapeDtypeStruct((2, 64, 128, 128), BF),
        in_specs=[vmem] * 2,
        out_specs=vmem,
        **settings(32, 1 << 29, 8),
    )(theta, theta_sib)
    one, flipped, blocks, dims, weights = lax.optimization_barrier(
        (one, flipped, blocks, dims, weights)
    )
    ones = [
        one,
        shift(one, "x", 1),
        shift(one, "x", -1),
        shift(one[:4], "x", 2),
        shift(one[4:], "x", -2),
    ]
    place = jnp.stack([(at_x + d) % 4 for d in (0, 3, 1, 2)]).astype(jnp.int32)

    left_own, _ = lax.optimization_barrier((left_own, ones[1:]))
    left_sib = swap(left_own)
    lefts = pl.pallas_call(
        left_kernel,
        out_shape=jax.ShapeDtypeStruct((2, *left_own.shape), BF),
        in_specs=[hbm] * 2,
        out_specs=vmem,
        scratch_shapes=[pltpu.SemaphoreType.DMA((2, 8))],
        **settings(32, 0, 8),
    )(left_own, left_sib)
    mine, other = pl.pallas_call(
        contract_kernel,
        out_shape=(jax.ShapeDtypeStruct((512, 128), BF),) * 2,
        in_specs=[smem] * 6 + [vmem] * 2 + [hbm] * 6,
        out_specs=(vmem, vmem),
        scratch_shapes=[
            pltpu.VMEM((8, 4, 8, 2, 48, 128), BF),
            pltpu.VMEM((4, 128, 2048), BF),
            pltpu.SemaphoreType.DMA((13,)),
        ],
        **settings(52, 1 << 30, 8),
    )(blocks // 24, blocks // 3 % 8, blocks % 3, weights, dims, place, flipped, lefts, two, *ones)

    mine = mine.reshape(64, 8, 128)
    other = swap(other).reshape(64, 8, 128)
    piece = jnp.concatenate(
        [jnp.where(first, mine, other), jnp.where(first, other, mine)], axis=1
    )
    pieces, owners = both_ways(piece, "y")
    place = jnp.stack([(at_y + o + 8) % 8 for o in owners]).astype(jnp.int32)
    return pl.pallas_call(
        finish_kernel,
        grid=(4,),
        out_shape=jax.ShapeDtypeStruct((64, 128, 128), BF),
        in_specs=[smem] + [pl.BlockSpec((16, 16, 128), lambda i: (i, 0, 0))] * 8,
        out_specs=pl.BlockSpec((16, 128, 128), lambda i: (i, 0, 0)),
        scratch_shapes=[pltpu.VMEM((16, 128, 128), BF)],
        compiler_params=pltpu.CompilerParams(vmem_limit_bytes=16 * 2**20),
        cost_estimate=pl.CostEstimate(flops=1 << 28, bytes_accessed=4 << 20, transcendentals=0),
    )(place, *pieces)


def solution(mesh):
    grid = Mesh(mesh.devices.reshape(8, 8, 4, 2), ("y", "z", "x", "c"))
    tensor = ("z", "x", "c")
    in_specs = (
        P(tensor, None, None),
        P("y", tensor, None, None),
        P("y", tensor, None, None),
        P("y", None),
        P(tensor),
        P(tensor),
        P(tensor, None),
        P(tensor),
    )
    return jax.shard_map(
        on_device, mesh=grid, in_specs=in_specs, out_specs=P(tensor, None, None), check_vma=False
    )
```

time: 194 us -> 184 us (0.948)
  waiting for transfers between devices: 90.7 us -> 58.1 us
  blocking collectives: 0 us -> 18.3 us
  local copies, waits for them, and re-layouts: 5.29 us -> 11.7 us
  other arithmetic: 4.3 us -> 2.06 us
  Pallas kernels: 17.4 us -> 19.5 us
    ppermute x4 -> x0, waiting for transfers between devices: 44 us -> none  [spread(): return lax.ppermute(x, (axis, 'c'), pairs)]
    all_to_all x0 -> x1, blocking collectives: none -> 18.3 us  [on_device(): lax.all_to_all(right, ('y', 'c'), split_axis=0, concat_axis=0, tiled=True)]
    ppermute x7 -> x11, waiting for transfers between devices: 18 us -> 35.9 us  [shift(): return lax.ppermute(x, axis, [(i, (i + by) % count) for i in range(count)])]
    ppermute x4 -> x0, starting transfers between devices: 15.4 us -> none  [spread(): return lax.ppermute(x, (axis, 'c'), pairs)]
    ppermute x7 -> x11, starting transfers between devices: 23 us -> 36.3 us  [shift(): return lax.ppermute(x, axis, [(i, (i + by) % count) for i in range(count)])]
    all_to_all x1 -> x2, waiting for transfers between devices: 22.7 us -> 15.2 us  [the longest x1 8.65 us: on_device(): two = lax.all_to_all(two, 'x', split_axis=0, concat_axis=0, tiled=True)]
    unnamed x39 -> x22, local copies, waits for them, and re-layouts: 2.1 us -> 8.9 us
    all_to_all x1 -> x2, starting transfers between devices: 10.6 us -> 14.8 us  [the longest x1 10.1 us: on_device(): one = lax.all_to_all(one, 'z', split_axis=0, concat_axis=0, tiled=True)]
  transfers between devices with their start and end apart: 19 -> 19, of which waited for: 12 -> 12; matrix products, arithmetic and copies ran while one was open for 1% -> 3% of each run, Pallas kernels for 0% -> 4%
where the time goes in v2:
time: 184 us; the launch traced here: 183 us
  starting transfers between devices  59.2 us (32%)
  waiting for transfers between devices  58.1 us (32%)
  Pallas kernels  19.5 us (11%)
  blocking collectives  18.3 us (10%)
  between operations  13.8 us (8%)
  local copies, waits for them, and re-layouts  11.7 us (6%)
  other arithmetic  2.06 us (1%)
    ppermute x11, starting transfers between devices, shift(): return lax.ppermute(x, axis, [(i, (i + by) % count) for i in range(count)])  36.3 us
    ppermute x11, waiting for transfers between devices, shift(): return lax.ppermute(x, axis, [(i, (i + by) % count) for i in range(count)])  35.9 us
    all_to_all x1, blocking collectives, on_device(): lax.all_to_all(right, ('y', 'c'), split_axis=0, concat_axis=0, tiled=True)  18.3 us
    all_to_all x1, starting transfers between devices, on_device(): one = lax.all_to_all(one, 'z', split_axis=0, concat_axis=0, tiled=True)  10.1 us
    unnamed x22, local copies, waits for them, and re-layouts  8.9 us
    pallas_call x1, Pallas kernels, on_device(): pl.pallas_call(contract_kernel, out_shape=(jax.ShapeDtypeStruct((512, 128...  8.86 us
    all_to_all x1, waiting for transfers between devices, on_device(): two = lax.all_to_all(two, 'x', split_axis=0, concat_axis=0, tiled=True)  8.65 us
    ppermute x4, starting transfers between devices, swap(): return lax.ppermute(x, 'c', [(0, 1), (1, 0)])  8.1 us
  transfers between devices with their start and end apart: 19, of which 12 were waited for; matrix products, arithmetic and copies ran while one was open for 3% of the time, Pallas kernels for 4%

profile of v2, /device:TPU:6, one launch (start us, length us, event | category | flops | bytes accessed | tf_op | source)
XLA Modules:
  0.0 182.7 jit_solution(8303133771411009707)
XLA Ops:
  10.0 18.3 %all_to_all.15 = bf16[16,64,128]{2,1,0:T(8,128)(2,1)S(1)} all-to-all(bf16[16,64,128]{2,1,0:T(8,128)(2,1)S(1)} %pad_maximum_fusion), channel_id=1, replica_groups=mesh['y'=8,'z'=8,'x'=4,'c'=2] {'y','c'}, dimensions={0} | all-to-all | bytes 524288 | tf_op jit(solution)/shard_map/all_to_all | solution.py:154
  29.2 4.8 %all-to-all-start.1 = ((bf16[4,8,2,32,128]{4,3,2,1,0:T(8,128)(2,1)}), bf16[4,8,2,32,128]{4,3,2,1,0:T(8,128)(2,1)S(1)}, u32[]{:S(2)}, u32[]{:S(2)}) async-start(bf16[4,8,2,32,128]{4,3,2,1,0:T(8,128)(2,1)} %broadcast_in_dim.21), calls=%async_computation.1 | async-start | bytes 1048576 | tf_op jit(solution)/shard_map/all_to_all | solution.py:158
  34.0 8.7 %all-to-all-done.1 = bf16[4,8,2,32,128]{4,3,2,1,0:T(8,128)(2,1)S(1)} async-done(((bf16[4,8,2,32,128]{4,3,2,1,0:T(8,128)(2,1)}), bf16[4,8,2,32,128]{4,3,2,1,0:T(8,128)(2,1)S(1)}, u32[]{:S(2)}, u32[]{:S(2)}) %all-to-all-start.1) | async-done | bytes 524320 | tf_op jit(solution)/shard_map/all_to_all | solution.py:158
  46.4 10.1 %all-to-all-start.2 = ((bf16[8,8,2,16,128]{4,3,2,1,0:T(8,128)(2,1)}), bf16[8,8,2,16,128]{4,3,2,1,0:T(8,128)(2,1)S(1)}, u32[]{:S(2)}, u32[]{:S(2)}) async-start(bf16[8,8,2,16,128]{4,3,2,1,0:T(8,128)(2,1)} %broadcast_in_dim.22), calls=%async_computation.2 | async-start | bytes 1048576 | tf_op jit(solution)/shard_map/all_to_all | solution.py:162
  56.5 2.1 %collective-permute-start.1 = (s32[2,64]{1,0:T(2,128)S(1)}, s32[2,64]{1,0:T(2,128)S(1)}, u32[]{:S(2)}, u32[]{:S(2)}) collective-permute-start(s32[2,64]{1,0:T(2,128)S(1)} %get-tuple-element.32), channel_id=1, source_target_pairs={{0,1},{1,0},{2,3},{3,2},{4,5},{5,4},{6,7},{7,6},{8,9},{9,8},{10,11... | collective-permute-start | bytes 1544 | tf_op jit(solution)/shard_map/ppermute | solution.py:30
  59.7 6.4 %shard_map.82.th_ref = bf16[2,64,128,128]{3,2,1,0:T(8,128)(2,1)S(1)} custom-call(bf16[64,128,128]{2,1,0:T(8,128)(2,1)S(1)} %copy-done.2, bf16[64,128,128]{2,1,0:T(8,128)(2,1)} %collective-permute-done.th_sib), custom_call_target="tpu_custom_call" | custom-call | flops 536870912 | bytes 8388608 | tf_op jit(solution)/shard_map/pallas_call | solution.py:178
  68.1 6.6 %all-to-all-done.2.rest_1_ = bf16[8,8,2,16,128]{4,3,2,1,0:T(8,128)(2,1)S(1)} async-done(((bf16[8,8,2,16,128]{4,3,2,1,0:T(8,128)(2,1)}), bf16[8,8,2,16,128]{4,3,2,1,0:T(8,128)(2,1)S(1)}, u32[]{:S(2)}, u32[]{:S(2)}) %all-to-all-start.2) | async-done | bytes 524320 | tf_op jit(solution)/shard_map/all_to_all | solution.py:162
  74.7 4.0 %collective-permute-start.2 = (bf16[8,8,2,16,128]{4,3,2,1,0:T(8,128)(2,1)S(1)}, bf16[8,8,2,16,128]{4,3,2,1,0:T(8,128)(2,1)S(1)}, u32[]{:S(2)}, u32[]{:S(2)}) collective-permute-start(bf16[8,8,2,16,128]{4,3,2,1,0:T(8,128)(2,1)S(1)} %all-to-all-done.2.rest_1_), channel_id=1, source_target_pairs={{0,2},{2,4},{4,6},{6,0},{1,3},{3,5},{5,7},{7,1},{8,10},{10,12},{12... | collective-permute-start | bytes 1572872 | tf_op jit(solution)/shard_map/ppermute | solution.py:16
  80.6 3.9 %collective-permute-start.4 = (bf16[4,8,2,16,128]{4,3,2,1,0:T(8,128)(2,1)S(1)}, bf16[4,8,2,16,128]{4,3,2,1,0:T(8,128)(2,1)S(1)}, u32[]{:S(2)}, u32[]{:S(2)}) collective-permute-start(bf16[4,8,2,16,128]{4,3,2,1,0:T(8,128)(2,1)S(1)} %get-tuple-element.26), channel_id=1, source_target_pairs={{0,4},{2,6},{4,0},{6,2},{1,5},{3,7},{5,1},{7,3},{8,12},{10,14},{12... | collective-permute-start | bytes 786440 | tf_op jit(solution)/shard_map/ppermute | solution.py:16
  84.5 3.4 %collective-permute-start.5 = (bf16[4,8,2,16,128]{4,3,2,1,0:T(8,128)(2,1)S(1)}, bf16[4,8,2,16,128]{4,3,2,1,0:T(8,128)(2,1)S(1)}, u32[]{:S(2)}, u32[]{:S(2)}) collective-permute-start(bf16[4,8,2,16,128]{4,3,2,1,0:T(8,128)(2,1)S(1)} %get-tuple-element.25), channel_id=1, source_target_pairs={{0,4},{2,6},{4,0},{6,2},{1,5},{3,7},{5,1},{7,3},{8,12},{10,14},{12... | collective-permute-start | bytes 786440 | tf_op jit(solution)/shard_map/ppermute | solution.py:16
  88.0 13.1 %collective-permute-done.4.rest_4_ = bf16[4,8,2,16,128]{4,3,2,1,0:T(8,128)(2,1)S(1)} collective-permute-done((bf16[4,8,2,16,128]{4,3,2,1,0:T(8,128)(2,1)S(1)}, bf16[4,8,2,16,128]{4,3,2,1,0:T(8,128)(2,1)S(1)}, u32[]{:S(2)}, u32[]{:S(2)}) %collective-permute-start.4) | collective-permute-done | bytes 262176 | tf_op jit(solution)/shard_map/ppermute | solution.py:16
  101.1 4.4 %collective-permute-done.5.rest_5_ = bf16[4,8,2,16,128]{4,3,2,1,0:T(8,128)(2,1)S(1)} collective-permute-done((bf16[4,8,2,16,128]{4,3,2,1,0:T(8,128)(2,1)S(1)}, bf16[4,8,2,16,128]{4,3,2,1,0:T(8,128)(2,1)S(1)}, u32[]{:S(2)}, u32[]{:S(2)}) %collective-permute-start.5) | collective-permute-done | bytes 262176 | tf_op jit(solution)/shard_map/ppermute | solution.py:16
  109.4 4.2 %collective-permute-done.6.l_sib = bf16[8,2,4,128,128]{4,3,2,1,0:T(8,128)(2,1)S(1)} collective-permute-done((bf16[8,2,4,128,128]{4,3,2,1,0:T(8,128)(2,1)}, bf16[8,2,4,128,128]{4,3,2,1,0:T(8,128)(2,1)S(1)}, u32[]{:S(2)}, u32[]{:S(2)}) %collective-permute-start.6) | collective-permute-done | bytes 2097184 | tf_op jit(solution)/shard_map/ppermute | solution.py:30
  118.7 8.9 %shard_map.84 = (bf16[512,128]{1,0:T(8,128)(2,1)S(1)}, bf16[512,128]{1,0:T(8,128)(2,1)S(1)}) custom-call(s32[2,64]{1,0:T(2,128)S(1)} %get-tuple-element.30.zi_ref, s32[2,64]{1,0:T(2,128)S(1)} %get-tuple-element.31.xc_ref, s32[2,64]{1,0:T(2,128)S(1)} %get-tuple-element.29.s_ref, f32[16,16]{1,0:T(8,128)S(1)} %add.141.c_ref, s32[2,4]{1,0:T(2,128)S(1)} %bitcast.43, ...), custom_call_target="tpu_custom_call" | custom-call | flops 1073741824 | bytes 8388608 | tf_op jit(solution)/shard_map/pallas_call | solution.py:207
  127.5 2.0 %collective-permute-start.7 = (bf16[512,128]{1,0:T(8,128)(2,1)S(1)}, bf16[512,128]{1,0:T(8,128)(2,1)S(1)}, u32[]{:S(2)}, u32[]{:S(2)}) collective-permute-start(bf16[512,128]{1,0:T(8,128)(2,1)S(1)} %get-tuple-element.24), channel_id=1, source_target_pairs={{0,1},{1,0},{2,3},{3,2},{4,5},{5,4},{6,7},{7,6},{8,9},{9,8},{10,11... | collective-permute-start | bytes 393224 | tf_op jit(solution)/shard_map/ppermute | solution.py:30
  130.8 2.8 %collective-permute-start.8 = (bf16[64,16,128]{2,1,0:T(8,128)(2,1)S(1)}, bf16[64,16,128]{2,1,0:T(8,128)(2,1)S(1)}, u32[]{:S(2)}, u32[]{:S(2)}) collective-permute-start(bf16[64,16,128]{2,1,0:T(8,128)(2,1)S(1)} %pad_maximum_fusion.1.refs_0_), channel_id=1, source_target_pairs={{0,64},{64,128},{128,192},{192,256},{256,320},{320,384},{384,448},... | collective-permute-start | bytes 786440 | tf_op jit(solution)/shard_map/ppermute | solution.py:16
  133.7 4.2 %collective-permute-start.9 = (bf16[64,16,128]{2,1,0:T(8,128)(2,1)S(1)}, bf16[64,16,128]{2,1,0:T(8,128)(2,1)S(1)}, u32[]{:S(2)}, u32[]{:S(2)}) collective-permute-start(bf16[64,16,128]{2,1,0:T(8,128)(2,1)S(1)} %pad_maximum_fusion.1.refs_0_), channel_id=1, source_target_pairs={{0,448},{64,0},{128,64},{192,128},{256,192},{320,256},{384,320},{4... | collective-permute-start | bytes 786440 | tf_op jit(solution)/shard_map/ppermute | solution.py:16
  137.9 4.4 %collective-permute-done.8.refs_1_ = bf16[64,16,128]{2,1,0:T(8,128)(2,1)S(1)} collective-permute-done((bf16[64,16,128]{2,1,0:T(8,128)(2,1)S(1)}, bf16[64,16,128]{2,1,0:T(8,128)(2,1)S(1)}, u32[]{:S(2)}, u32[]{:S(2)}) %collective-permute-start.8) | collective-permute-done | bytes 262176 | tf_op jit(solution)/shard_map/ppermute | solution.py:16
  144.2 5.1 %collective-permute-start.11 = (bf16[64,16,128]{2,1,0:T(8,128)(2,1)S(1)}, bf16[64,16,128]{2,1,0:T(8,128)(2,1)S(1)}, u32[]{:S(2)}, u32[]{:S(2)}) collective-permute-start(bf16[64,16,128]{2,1,0:T(8,128)(2,1)S(1)} %collective-permute-done.9.refs_2_), channel_id=1, source_target_pairs={{0,448},{64,0},{128,64},{192,128},{256,192},{320,256},{384,320},{4... | collective-permute-start | bytes 786440 | tf_op jit(solution)/shard_map/ppermute | solution.py:16
  149.4 3.6 %collective-permute-done.10.refs_3_ = bf16[64,16,128]{2,1,0:T(8,128)(2,1)S(1)} collective-permute-done((bf16[64,16,128]{2,1,0:T(8,128)(2,1)S(1)}, bf16[64,16,128]{2,1,0:T(8,128)(2,1)S(1)}, u32[]{:S(2)}, u32[]{:S(2)}) %collective-permute-start.10) | collective-permute-done | bytes 262176 | tf_op jit(solution)/shard_map/ppermute | solution.py:16
  154.9 5.1 %collective-permute-start.13 = (bf16[64,16,128]{2,1,0:T(8,128)(2,1)S(1)}, bf16[64,16,128]{2,1,0:T(8,128)(2,1)S(1)}, u32[]{:S(2)}, u32[]{:S(2)}) collective-permute-start(bf16[64,16,128]{2,1,0:T(8,128)(2,1)S(1)} %collective-permute-done.11.refs_4_), channel_id=1, source_target_pairs={{0,448},{64,0},{128,64},{192,128},{256,192},{320,256},{384,320},{4... | collective-permute-start | bytes 786440 | tf_op jit(solution)/shard_map/ppermute | solution.py:16
  160.0 2.6 %collective-permute-done.12.refs_5_ = bf16[64,16,128]{2,1,0:T(8,128)(2,1)S(1)} collective-permute-done((bf16[64,16,128]{2,1,0:T(8,128)(2,1)S(1)}, bf16[64,16,128]{2,1,0:T(8,128)(2,1)S(1)}, u32[]{:S(2)}, u32[]{:S(2)}) %collective-permute-start.12) | collective-permute-done | bytes 262176 | tf_op jit(solution)/shard_map/ppermute | solution.py:16
  164.7 7.4 %collective-permute-done.14.refs_7_ = bf16[64,16,128]{2,1,0:T(8,128)(2,1)S(1)} collective-permute-done((bf16[64,16,128]{2,1,0:T(8,128)(2,1)S(1)}, bf16[64,16,128]{2,1,0:T(8,128)(2,1)S(1)}, u32[]{:S(2)}, u32[]{:S(2)}) %collective-permute-start.14) | collective-permute-done | bytes 262176 | tf_op jit(solution)/shard_map/ppermute | solution.py:16
  172.1 3.8 %shard_map.85 = bf16[64,128,128]{2,1,0:T(8,128)(2,1)} custom-call(s32[8]{0:T(128)S(1)} %stack.68.place_ref, bf16[64,16,128]{2,1,0:T(8,128)(2,1)S(1)} %pad_maximum_fusion.1.refs_0_, bf16[64,16,128]{2,1,0:T(8,128)(2,1)S(1)} %collective-permute-done.8.refs_1_, bf16[64,16,128]{2,1,0:T(8,128)(2,1)S(1)} %collective-permute-done.9.refs_2_, ...), custom_call_target="tpu_custom_call" | custom-call | flops 268435456 | bytes 4194304 | tf_op jit(solution)/shard_map/pallas_call | solution.py:227
  (69 shorter events, 29.0 us)
Async XLA Ops:
  6.5 100.0 %all-gather.5.cloned.1.call-start = ((), (), s32[]{:S(2)}) async-start(), calls=%async_computation.3 | async-start | bytes 2359296 | tf_op jit(solution)/shard_map/all_gather | solution.py:153
  9.8 33.6 %copy-start.2 = (bf16[64,128,128]{2,1,0:T(8,128)(2,1)S(1)}, bf16[64,128,128]{2,1,0:T(8,128)(2,1)}, u32[]{:S(2)}) copy-start(bf16[64,128,128]{2,1,0:T(8,128)(2,1)} %th_own.1) | copy-start | bytes 6291460
  28.3 28.2 %copy-start.8 = (s32[64]{0:T(128)S(1)}, s32[64]{0:T(128)}, u32[]{:S(2)}) copy-start(s32[64]{0:T(128)} %param.15) | copy-start | bytes 772
  28.3 28.2 %copy-start.9 = (s32[64,1]{0,1:T(1,128)S(1)}, s32[64,1]{0,1:T(1,128)}, u32[]{:S(2)}) copy-start(s32[64,1]{0,1:T(1,128)} %param.14) | copy-start | bytes 772
  28.3 28.2 %copy-start.10 = (s32[4]{0:T(128)S(1)}, s32[4]{0:T(128)}, u32[]{:S(2)}) copy-start(s32[4]{0:T(128)} %param.12) | copy-start | bytes 52
  29.2 13.4 %all-to-all-start.1 = ((bf16[4,8,2,32,128]{4,3,2,1,0:T(8,128)(2,1)}), bf16[4,8,2,32,128]{4,3,2,1,0:T(8,128)(2,1)S(1)}, u32[]{:S(2)}, u32[]{:S(2)}) async-start(bf16[4,8,2,32,128]{4,3,2,1,0:T(8,128)(2,1)} %broadcast_in_dim.21), calls=%async_computation.1 | async-start | bytes 1048576 | tf_op jit(solution)/shard_map/all_to_all | solution.py:158
  34.0 83.7 %all-gather.7.cloned.1.call-start = ((), (), s32[]{:S(2)}) async-start(), calls=%async_computation.4 | async-start | bytes 4718592 | tf_op jit(solution)/shard_map/all_gather | solution.py:160
  43.5 16.2 %collective-permute-start = (bf16[64,128,128]{2,1,0:T(8,128)(2,1)S(1)}, bf16[64,128,128]{2,1,0:T(8,128)(2,1)}, u32[]{:S(2)}, u32[]{:S(2)}) collective-permute-start(bf16[64,128,128]{2,1,0:T(8,128)(2,1)S(1)} %copy-done.2), channel_id=1, source_target_pairs={{0,1},{1,0},{2,3},{3,2},{4,5},{5,4},{6,7},{7,6},{8,9},{9,8},{10,11... | collective-permute-start | bytes 6291464 | tf_op jit(solution)/shard_map/ppermute | solution.py:30
  46.4 28.3 %all-to-all-start.2 = ((bf16[8,8,2,16,128]{4,3,2,1,0:T(8,128)(2,1)}), bf16[8,8,2,16,128]{4,3,2,1,0:T(8,128)(2,1)S(1)}, u32[]{:S(2)}, u32[]{:S(2)}) async-start(bf16[8,8,2,16,128]{4,3,2,1,0:T(8,128)(2,1)} %broadcast_in_dim.22), calls=%async_computation.2 | async-start | bytes 1048576 | tf_op jit(solution)/shard_map/all_to_all | solution.py:162
  56.5 3.0 %collective-permute-start.1 = (s32[2,64]{1,0:T(2,128)S(1)}, s32[2,64]{1,0:T(2,128)S(1)}, u32[]{:S(2)}, u32[]{:S(2)}) collective-permute-start(s32[2,64]{1,0:T(2,128)S(1)} %get-tuple-element.32), channel_id=1, source_target_pairs={{0,1},{1,0},{2,3},{3,2},{4,5},{5,4},{6,7},{7,6},{8,9},{9,8},{10,11... | collective-permute-start | bytes 1544 | tf_op jit(solution)/shard_map/ppermute | solution.py:30
  66.1 2.0 %copy-start = (bf16[2,64,128,128]{3,2,1,0:T(8,128)(2,1)}, bf16[2,64,128,128]{3,2,1,0:T(8,128)(2,1)S(1)}, u32[]{:S(2)}) copy-start(bf16[2,64,128,128]{3,2,1,0:T(8,128)(2,1)S(1)} %shard_map.82.th_ref) | copy-start | bytes 12582916
  74.7 31.5 %collective-permute-start.2 = (bf16[8,8,2,16,128]{4,3,2,1,0:T(8,128)(2,1)S(1)}, bf16[8,8,2,16,128]{4,3,2,1,0:T(8,128)(2,1)S(1)}, u32[]{:S(2)}, u32[]{:S(2)}) collective-permute-start(bf16[8,8,2,16,128]{4,3,2,1,0:T(8,128)(2,1)S(1)} %all-to-all-done.2.rest_1_), channel_id=1, source_target_pairs={{0,2},{2,4},{4,6},{6,0},{1,3},{3,5},{5,7},{7,1},{8,10},{10,12},{12... | collective-permute-start | bytes 1572872 | tf_op jit(solution)/shard_map/ppermute | solution.py:16
  78.6 27.9 %collective-permute-start.3 = (bf16[8,8,2,16,128]{4,3,2,1,0:T(8,128)(2,1)S(1)}, bf16[8,8,2,16,128]{4,3,2,1,0:T(8,128)(2,1)S(1)}, u32[]{:S(2)}, u32[]{:S(2)}) collective-permute-start(bf16[8,8,2,16,128]{4,3,2,1,0:T(8,128)(2,1)S(1)} %all-to-all-done.2.rest_1_), channel_id=1, source_target_pairs={{0,6},{2,0},{4,2},{6,4},{1,7},{3,1},{5,3},{7,5},{8,14},{10,8},{12,... | collective-permute-start | bytes 1572872 | tf_op jit(solution)/shard_map/ppermute | solution.py:16
  80.6 20.5 %collective-permute-start.4 = (bf16[4,8,2,16,128]{4,3,2,1,0:T(8,128)(2,1)S(1)}, bf16[4,8,2,16,128]{4,3,2,1,0:T(8,128)(2,1)S(1)}, u32[]{:S(2)}, u32[]{:S(2)}) collective-permute-start(bf16[4,8,2,16,128]{4,3,2,1,0:T(8,128)(2,1)S(1)} %get-tuple-element.26), channel_id=1, source_target_pairs={{0,4},{2,6},{4,0},{6,2},{1,5},{3,7},{5,1},{7,3},{8,12},{10,14},{12... | collective-permute-start | bytes 786440 | tf_op jit(solution)/shard_map/ppermute | solution.py:16
  84.5 20.9 %collective-permute-start.5 = (bf16[4,8,2,16,128]{4,3,2,1,0:T(8,128)(2,1)S(1)}, bf16[4,8,2,16,128]{4,3,2,1,0:T(8,128)(2,1)S(1)}, u32[]{:S(2)}, u32[]{:S(2)}) collective-permute-start(bf16[4,8,2,16,128]{4,3,2,1,0:T(8,128)(2,1)S(1)} %get-tuple-element.25), channel_id=1, source_target_pairs={{0,4},{2,6},{4,0},{6,2},{1,5},{3,7},{5,1},{7,3},{8,12},{10,14},{12... | collective-permute-start | bytes 786440 | tf_op jit(solution)/shard_map/ppermute | solution.py:16
  107.4 6.3 %collective-permute-start.6 = (bf16[8,2,4,128,128]{4,3,2,1,0:T(8,128)(2,1)}, bf16[8,2,4,128,128]{4,3,2,1,0:T(8,128)(2,1)S(1)}, u32[]{:S(2)}, u32[]{:S(2)}) collective-permute-start(bf16[8,2,4,128,128]{4,3,2,1,0:T(8,128)(2,1)} %bitcast.41), channel_id=1, source_target_pairs={{0,1},{1,0},{2,3},{3,2},{4,5},{5,4},{6,7},{7,6},{8,9},{9,8},{10,11... | collective-permute-start | bytes 6291464 | tf_op jit(solution)/shard_map/ppermute | solution.py:30
  127.5 3.2 %collective-permute-start.7 = (bf16[512,128]{1,0:T(8,128)(2,1)S(1)}, bf16[512,128]{1,0:T(8,128)(2,1)S(1)}, u32[]{:S(2)}, u32[]{:S(2)}) collective-permute-start(bf16[512,128]{1,0:T(8,128)(2,1)S(1)} %get-tuple-element.24), channel_id=1, source_target_pairs={{0,1},{1,0},{2,3},{3,2},{4,5},{5,4},{6,7},{7,6},{8,9},{9,8},{10,11... | collective-permute-start | bytes 393224 | tf_op jit(solution)/shard_map/ppermute | solution.py:30
  130.8 11.5 %collective-permute-start.8 = (bf16[64,16,128]{2,1,0:T(8,128)(2,1)S(1)}, bf16[64,16,128]{2,1,0:T(8,128)(2,1)S(1)}, u32[]{:S(2)}, u32[]{:S(2)}) collective-permute-start(bf16[64,16,128]{2,1,0:T(8,128)(2,1)S(1)} %pad_maximum_fusion.1.refs_0_), channel_id=1, source_target_pairs={{0,64},{64,128},{128,192},{192,256},{256,320},{320,384},{384,448},... | collective-permute-start | bytes 786440 | tf_op jit(solution)/shard_map/ppermute | solution.py:16
  133.7 10.5 %collective-permute-start.9 = (bf16[64,16,128]{2,1,0:T(8,128)(2,1)S(1)}, bf16[64,16,128]{2,1,0:T(8,128)(2,1)S(1)}, u32[]{:S(2)}, u32[]{:S(2)}) collective-permute-start(bf16[64,16,128]{2,1,0:T(8,128)(2,1)S(1)} %pad_maximum_fusion.1.refs_0_), channel_id=1, source_target_pairs={{0,448},{64,0},{128,64},{192,128},{256,192},{320,256},{384,320},{4... | collective-permute-start | bytes 786440 | tf_op jit(solution)/shard_map/ppermute | solution.py:16
  142.3 10.6 %collective-permute-start.10 = (bf16[64,16,128]{2,1,0:T(8,128)(2,1)S(1)}, bf16[64,16,128]{2,1,0:T(8,128)(2,1)S(1)}, u32[]{:S(2)}, u32[]{:S(2)}) collective-permute-start(bf16[64,16,128]{2,1,0:T(8,128)(2,1)S(1)} %collective-permute-done.8.refs_1_), channel_id=1, source_target_pairs={{0,64},{64,128},{128,192},{192,256},{256,320},{320,384},{384,448},... | collective-permute-start | bytes 786440 | tf_op jit(solution)/shard_map/ppermute | solution.py:16
  144.2 10.6 %collective-permute-start.11 = (bf16[64,16,128]{2,1,0:T(8,128)(2,1)S(1)}, bf16[64,16,128]{2,1,0:T(8,128)(2,1)S(1)}, u32[]{:S(2)}, u32[]{:S(2)}) collective-permute-start(bf16[64,16,128]{2,1,0:T(8,128)(2,1)S(1)} %collective-permute-done.9.refs_2_), channel_id=1, source_target_pairs={{0,448},{64,0},{128,64},{192,128},{256,192},{320,256},{384,320},{4... | collective-permute-start | bytes 786440 | tf_op jit(solution)/shard_map/ppermute | solution.py:16
  152.9 9.7 %collective-permute-start.12 = (bf16[64,16,128]{2,1,0:T(8,128)(2,1)S(1)}, bf16[64,16,128]{2,1,0:T(8,128)(2,1)S(1)}, u32[]{:S(2)}, u32[]{:S(2)}) collective-permute-start(bf16[64,16,128]{2,1,0:T(8,128)(2,1)S(1)} %collective-permute-done.10.refs_3_), channel_id=1, source_target_pairs={{0,64},{64,128},{128,192},{192,256},{256,320},{320,384},{384,448},... | collective-permute-start | bytes 786440 | tf_op jit(solution)/shard_map/ppermute | solution.py:16
  154.9 9.9 %collective-permute-start.13 = (bf16[64,16,128]{2,1,0:T(8,128)(2,1)S(1)}, bf16[64,16,128]{2,1,0:T(8,128)(2,1)S(1)}, u32[]{:S(2)}, u32[]{:S(2)}) collective-permute-start(bf16[64,16,128]{2,1,0:T(8,128)(2,1)S(1)} %collective-permute-done.11.refs_4_), channel_id=1, source_target_pairs={{0,448},{64,0},{128,64},{192,128},{256,192},{320,256},{384,320},{4... | collective-permute-start | bytes 786440 | tf_op jit(solution)/shard_map/ppermute | solution.py:16
  162.6 9.5 %collective-permute-start.14 = (bf16[64,16,128]{2,1,0:T(8,128)(2,1)S(1)}, bf16[64,16,128]{2,1,0:T(8,128)(2,1)S(1)}, u32[]{:S(2)}, u32[]{:S(2)}) collective-permute-start(bf16[64,16,128]{2,1,0:T(8,128)(2,1)S(1)} %collective-permute-done.12.refs_5_), channel_id=1, source_target_pairs={{0,64},{64,128},{128,192},{192,256},{256,320},{320,384},{384,448},... | collective-permute-start | bytes 786440 | tf_op jit(solution)/shard_map/ppermute | solution.py:16
  (6 other events, 6.9 us)
Sparse Core Ops, SparseCore 0:
  9.4 48.0 all-gather.4
  59.6 57.4 all-gather.6

commit v3 on v2

--- a/solution.py
+++ b/solution.py
@@ -6,6 +6,7 @@
 from jax.sharding import Mesh, PartitionSpec as P
 
 PHYS = 16
+SPLIT = 7
 NT = (((1,), (1,)), ((), ()))
 BF = jnp.bfloat16
 F32 = jnp.float32
@@ -46,21 +47,9 @@
                 out_ref[half, i * 8 + k] = flip(th[i * 8 + k])
 
 
-def left_kernel(l_own, l_sib, out_ref, sems):
-    copies = [
-        pltpu.make_async_copy(ref.at[y], out_ref.at[half, y], sems.at[half, y])
-        for half, ref in enumerate((l_own, l_sib))
-        for y in range(8)
-    ]
-    for copy in copies:
-        copy.start()
-    for copy in copies:
-        copy.wait()
-
-
-def contract_kernel(zi_ref, xc_ref, s_ref, c_ref, dims_ref, place_ref, th_ref, l_ref, *rest):
-    two, one = rest[0], rest[1:6]
-    out_refs, (r_ref, a_ref, sems) = rest[6:8], rest[8:]
+def contract_kernel(zi_ref, xc_ref, s_ref, c_ref, dims_ref, place_ref, *rest):
+    theta, lefts, two, one = rest[0], rest[1:3], rest[3], rest[4:9]
+    out_refs, (r_ref, th_ref, l_ref, a_ref, sems) = rest[9:11], rest[11:]
     copies = []
 
     def fetch(src, dst):
@@ -69,25 +58,30 @@
         copies.append(copy)
 
     for z in range(8):
-        fetch(two.at[z], r_ref.at[z, :, :, :, pl.ds(0, 32)])
-    for d in range(3):
-        fetch(one[d], r_ref.at[:, place_ref[d], :, :, pl.ds(32, 16)])
-    for d in range(2):
-        fetch(one[3 + d], r_ref.at[pl.ds(4 * d, 4), place_ref[3], :, :, pl.ds(32, 16)])
-    for copy in copies:
-        copy.wait()
+        fetch(two.at[z, :, pl.ds(0, 8)], r_ref.at[z, :, 0])
+        fetch(two.at[z, :, pl.ds(8, SPLIT)], r_ref.at[z, :, 1, pl.ds(0, SPLIT)])
+    for d in range(5):
+        z = pl.ds(4 * (d - 3), 4) if d > 2 else pl.ds(0, 8)
+        x = place_ref[min(d, 3)]
+        fetch(one[d].at[:, pl.ds(0, 8)], r_ref.at[z, x, 2])
+        fetch(one[d].at[:, pl.ds(8, 8 - SPLIT)], r_ref.at[z, x, 1, pl.ds(SPLIT, 8 - SPLIT)])
+    for half in range(2):
+        fetch(theta.at[half], th_ref.at[half])
+        fetch(lefts[half], l_ref.at[half])
 
     lane = lax.broadcasted_iota(jnp.int32, (128, 128), 1)
     for half in range(2):
+        for copy in copies[28 * half : 28 + 2 * half]:
+            copy.wait()
+
         @pl.loop(0, 4, unroll=4)
         def sector(s):
             for pp in range(PHYS // 2):
                 prods = []
                 for e in range(2):
                     n = s * PHYS + 2 * pp + e
-                    row = pl.multiple_of(s_ref[half, n] * 16, 16)
                     xc = xc_ref[half, n]
-                    tile = r_ref[zi_ref[half, n], xc // 2, :, xc % 2, pl.ds(row, 16)]
+                    tile = r_ref[zi_ref[half, n], xc // 2, s_ref[half, n], :, xc % 2]
                     prods.append(
                         jnp.dot(
                             tile.reshape(128, 128), th_ref[half, n], preferred_element_type=F32
@@ -154,11 +148,13 @@
     right = lax.all_to_all(
         right, ("y", "c"), split_axis=0, concat_axis=0, tiled=True
     ).reshape(8, 2, 64, 128)
-    two = jnp.broadcast_to(right[None, :, :, :32], (4, 8, 2, 32, 128))
+    two = jnp.concatenate([right[:, :, :16], right[:SPLIT, :, 16:32]], axis=0)
+    one = jnp.concatenate([right[:, :, 32:48], right[SPLIT:, :, 16:32]], axis=0)
+    two = jnp.broadcast_to(two[None], (4, *two.shape))
     two = lax.all_to_all(two, "x", split_axis=0, concat_axis=0, tiled=True)
-    one, two = lax.optimization_barrier((right[:, :, 32:48], two))
+    one, two = lax.optimization_barrier((one, two))
     two = lax.all_gather(two, "z")
-    one = jnp.broadcast_to(one[None], (8, 8, 2, 16, 128))
+    one = jnp.broadcast_to(one[None], (8, *one.shape))
     one = lax.all_to_all(one, "z", split_axis=0, concat_axis=0, tiled=True)
     theta_sib = swap(theta)
     weights = right[:, 0, 48:51, :32].astype(F32)
@@ -194,28 +190,22 @@
     ]
     place = jnp.stack([(at_x + d) % 4 for d in (0, 3, 1, 2)]).astype(jnp.int32)
 
-    left_own, _ = lax.optimization_barrier((left_own, ones[1:]))
+    left_own, _ = lax.optimization_barrier((left_own, one))
     left_sib = swap(left_own)
-    lefts = pl.pallas_call(
-        left_kernel,
-        out_shape=jax.ShapeDtypeStruct((2, *left_own.shape), BF),
-        in_specs=[hbm] * 2,
-        out_specs=vmem,
-        scratch_shapes=[pltpu.SemaphoreType.DMA((2, 8))],
-        **settings(32, 0, 8),
-    )(left_own, left_sib)
     mine, other = pl.pallas_call(
         contract_kernel,
         out_shape=(jax.ShapeDtypeStruct((512, 128), BF),) * 2,
-        in_specs=[smem] * 6 + [vmem] * 2 + [hbm] * 6,
+        in_specs=[smem] * 6 + [hbm] * 9,
         out_specs=(vmem, vmem),
         scratch_shapes=[
-            pltpu.VMEM((8, 4, 8, 2, 48, 128), BF),
+            pltpu.VMEM((8, 4, 3, 8, 2, 16, 128), BF),
+            pltpu.VMEM((2, 64, 128, 128), BF),
+            pltpu.VMEM((2, 8, 2, 4, 128, 128), BF),
             pltpu.VMEM((4, 128, 2048), BF),
-            pltpu.SemaphoreType.DMA((13,)),
+            pltpu.SemaphoreType.DMA((30,)),
         ],
-        **settings(52, 1 << 30, 8),
-    )(blocks // 24, blocks // 3 % 8, blocks % 3, weights, dims, place, flipped, lefts, two, *ones)
+        **settings(56, 1 << 30, 8),
+    )(blocks // 24, blocks // 3 % 8, blocks % 3, weights, dims, place, flipped, left_own, left_sib, two, *ones)
 
     mine = mine.reshape(64, 8, 128)
     other = swap(other).reshape(64, 8, 128)
@@ -226,11 +216,11 @@
     place = jnp.stack([(at_y + o + 8) % 8 for o in owners]).astype(jnp.int32)
     return pl.pallas_call(
         finish_kernel,
-        grid=(4,),
+        grid=(2,),
         out_shape=jax.ShapeDtypeStruct((64, 128, 128), BF),
-        in_specs=[smem] + [pl.BlockSpec((16, 16, 128), lambda i: (i, 0, 0))] * 8,
-        out_specs=pl.BlockSpec((16, 128, 128), lambda i: (i, 0, 0)),
-        scratch_shapes=[pltpu.VMEM((16, 128, 128), BF)],
+        in_specs=[smem] + [pl.BlockSpec((32, 16, 128), lambda i: (i, 0, 0))] * 8,
+        out_specs=pl.BlockSpec((32, 128, 128), lambda i: (i, 0, 0)),
+        scratch_shapes=[pltpu.VMEM((32, 128, 128), BF)],
         compiler_params=pltpu.CompilerParams(vmem_limit_bytes=16 * 2**20),
         cost_estimate=pl.CostEstimate(flops=1 << 28, bytes_accessed=4 << 20, transcendentals=0),
     )(place, *pieces)

time: 184 us -> 181 us (0.984)
  local copies, waits for them, and re-layouts: 11.7 us -> 6.2 us
  other arithmetic: 2.06 us -> 4.7 us
    unnamed x22, local copies, waits for them, and re-layouts: 8.9 us -> 2.82 us
    all_gather x1, waiting for transfers between devices: 0.01 us -> 4.37 us  [on_device(): two = lax.all_gather(two, 'z')]
    ppermute x4, waiting for transfers between devices: 6.29 us -> 2.42 us  [swap(): return lax.ppermute(x, 'c', [(0, 1), (1, 0)])]
    pallas_call x2 -> x1, Pallas kernels: 4.25 us -> 3.5 us  [on_device(): pl.pallas_call(finish_kernel, grid=(2,), out_shape=jax.ShapeDtypeStruct((...]
  transfers between devices with their start and end apart: 19 -> 19, of which waited for: 12 -> 12; matrix products, arithmetic and copies ran while one was open for 3% -> 4% of each run, Pallas kernels for 4% -> 4%
where the time goes in v3:
time: 181 us; the launch traced here: 180 us
  starting transfers between devices  60.3 us (33%)
  waiting for transfers between devices  57.5 us (32%)
  Pallas kernels  19.3 us (11%)
  blocking collectives  18.3 us (10%)
  between operations  13.9 us (8%)
  local copies, waits for them, and re-layouts  6.2 us (3%)
  other arithmetic  4.7 us (3%)
    ppermute x11, starting transfers between devices, shift(): return lax.ppermute(x, axis, [(i, (i + by) % count) for i in range(count)])  37.4 us
    ppermute x11, waiting for transfers between devices, shift(): return lax.ppermute(x, axis, [(i, (i + by) % count) for i in range(count)])  34.8 us
    all_to_all x1, blocking collectives, on_device(): lax.all_to_all(right, ('y', 'c'), split_axis=0, concat_axis=0, tiled=True)  18.3 us
    all_to_all x1, starting transfers between devices, on_device(): one = lax.all_to_all(one, 'z', split_axis=0, concat_axis=0, tiled=True)  10.1 us
    pallas_call x1, Pallas kernels, on_device(): pl.pallas_call(contract_kernel, out_shape=(jax.ShapeDtypeStruct((512, 128...  9.35 us
    all_to_all x1, waiting for transfers between devices, on_device(): two = lax.all_to_all(two, 'x', split_axis=0, concat_axis=0, tiled=True)  8.3 us
    ppermute x4, starting transfers between devices, swap(): return lax.ppermute(x, 'c', [(0, 1), (1, 0)])  8.01 us
    all_to_all x1, waiting for transfers between devices, on_device(): one = lax.all_to_all(one, 'z', split_axis=0, concat_axis=0, tiled=True)  6.88 us
  transfers between devices with their start and end apart: 19, of which 12 were waited for; matrix products, arithmetic and copies ran while one was open for 4% of the time, Pallas kernels for 4%

profile of v3, /device:TPU:6, one launch (start us, length us, event | category | flops | bytes accessed | tf_op | source)
XLA Modules:
  0.0 180.1 jit_solution(13360450306961068663)
XLA Ops:
  10.0 18.3 %all_to_all.15 = bf16[16,64,128]{2,1,0:T(8,128)(2,1)S(1)} all-to-all(bf16[16,64,128]{2,1,0:T(8,128)(2,1)S(1)} %pad_maximum_fusion), channel_id=1, replica_groups=mesh['y'=8,'z'=8,'x'=4,'c'=2] {'y','c'}, dimensions={0} | all-to-all | bytes 524288 | tf_op jit(solution)/shard_map/all_to_all | solution.py:148
  29.2 4.8 %all-to-all-start.1 = ((bf16[4,15,2,16,128]{4,3,2,1,0:T(8,128)(2,1)}), bf16[4,15,2,16,128]{4,3,2,1,0:T(8,128)(2,1)S(1)}, u32[]{:S(2)}, u32[]{:S(2)}) async-start(bf16[4,15,2,16,128]{4,3,2,1,0:T(8,128)(2,1)} %broadcast_in_dim.21), calls=%async_computation.1 | async-start | bytes 983040 | tf_op jit(solution)/shard_map/all_to_all | solution.py:154
  34.0 8.3 %all-to-all-done.1 = bf16[4,15,2,16,128]{4,3,2,1,0:T(8,128)(2,1)S(1)} async-done(((bf16[4,15,2,16,128]{4,3,2,1,0:T(8,128)(2,1)}), bf16[4,15,2,16,128]{4,3,2,1,0:T(8,128)(2,1)S(1)}, u32[]{:S(2)}, u32[]{:S(2)}) %all-to-all-start.1) | async-done | bytes 491552 | tf_op jit(solution)/shard_map/all_to_all | solution.py:154
  46.0 10.1 %all-to-all-start.2 = ((bf16[8,9,2,16,128]{4,3,2,1,0:T(8,128)(2,1)}), bf16[8,9,2,16,128]{4,3,2,1,0:T(8,128)(2,1)S(1)}, u32[]{:S(2)}, u32[]{:S(2)}) async-start(bf16[8,9,2,16,128]{4,3,2,1,0:T(8,128)(2,1)} %broadcast_in_dim.22), calls=%async_computation.2 | async-start | bytes 1179648 | tf_op jit(solution)/shard_map/all_to_all | solution.py:158
  56.2 2.1 %collective-permute-start.1 = (s32[2,64]{1,0:T(2,128)S(1)}, s32[2,64]{1,0:T(2,128)S(1)}, u32[]{:S(2)}, u32[]{:S(2)}) collective-permute-start(s32[2,64]{1,0:T(2,128)S(1)} %get-tuple-element.34), channel_id=1, source_target_pairs={{0,1},{1,0},{2,3},{3,2},{4,5},{5,4},{6,7},{7,6},{8,9},{9,8},{10,11... | collective-permute-start | bytes 1544 | tf_op jit(solution)/shard_map/ppermute | solution.py:31
  60.5 6.4 %shard_map.82.rest_0_ = bf16[2,64,128,128]{3,2,1,0:T(8,128)(2,1)S(1)} custom-call(bf16[64,128,128]{2,1,0:T(8,128)(2,1)S(1)} %copy-done.1, bf16[64,128,128]{2,1,0:T(8,128)(2,1)} %collective-permute-done.th_sib), custom_call_target="tpu_custom_call" | custom-call | flops 536870912 | bytes 8388608 | tf_op jit(solution)/shard_map/pallas_call | solution.py:174
  68.9 6.9 %all-to-all-done.2.rest_4_ = bf16[8,9,2,16,128]{4,3,2,1,0:T(8,128)(2,1)S(1)} async-done(((bf16[8,9,2,16,128]{4,3,2,1,0:T(8,128)(2,1)}), bf16[8,9,2,16,128]{4,3,2,1,0:T(8,128)(2,1)S(1)}, u32[]{:S(2)}, u32[]{:S(2)}) %all-to-all-start.2) | async-done | bytes 589856 | tf_op jit(solution)/shard_map/all_to_all | solution.py:158
  79.6 5.1 %collective-permute-start.3 = (bf16[8,9,2,16,128]{4,3,2,1,0:T(8,128)(2,1)S(1)}, bf16[8,9,2,16,128]{4,3,2,1,0:T(8,128)(2,1)}, u32[]{:S(2)}, u32[]{:S(2)}) collective-permute-start(bf16[8,9,2,16,128]{4,3,2,1,0:T(8,128)(2,1)S(1)} %all-to-all-done.2.rest_4_), channel_id=1, source_target_pairs={{0,2},{2,4},{4,6},{6,0},{1,3},{3,5},{5,7},{7,1},{8,10},{10,12},{12... | collective-permute-start | bytes 1769480 | tf_op jit(solution)/shard_map/ppermute | solution.py:17
  84.9 2.8 %collective-permute-start.6 = (bf16[4,9,2,16,128]{4,3,2,1,0:T(8,128)(2,1)S(1)}, bf16[4,9,2,16,128]{4,3,2,1,0:T(8,128)(2,1)S(1)}, u32[]{:S(2)}, u32[]{:S(2)}) collective-permute-start(bf16[4,9,2,16,128]{4,3,2,1,0:T(8,128)(2,1)S(1)} %get-tuple-element.25), channel_id=1, source_target_pairs={{0,4},{2,6},{4,0},{6,2},{1,5},{3,7},{5,1},{7,3},{8,12},{10,14},{12... | collective-permute-start | bytes 884744 | tf_op jit(solution)/shard_map/ppermute | solution.py:17
  87.7 4.6 %collective-permute-start.5 = (bf16[4,9,2,16,128]{4,3,2,1,0:T(8,128)(2,1)S(1)}, bf16[4,9,2,16,128]{4,3,2,1,0:T(8,128)(2,1)S(1)}, u32[]{:S(2)}, u32[]{:S(2)}) collective-permute-start(bf16[4,9,2,16,128]{4,3,2,1,0:T(8,128)(2,1)S(1)} %get-tuple-element.26), channel_id=1, source_target_pairs={{0,4},{2,6},{4,0},{6,2},{1,5},{3,7},{5,1},{7,3},{8,12},{10,14},{12... | collective-permute-start | bytes 884744 | tf_op jit(solution)/shard_map/ppermute | solution.py:17
  93.5 10.0 %collective-permute-done.6.rest_8_ = bf16[4,9,2,16,128]{4,3,2,1,0:T(8,128)(2,1)S(1)} collective-permute-done((bf16[4,9,2,16,128]{4,3,2,1,0:T(8,128)(2,1)S(1)}, bf16[4,9,2,16,128]{4,3,2,1,0:T(8,128)(2,1)S(1)}, u32[]{:S(2)}, u32[]{:S(2)}) %collective-permute-start.6) | collective-permute-done | bytes 294944 | tf_op jit(solution)/shard_map/ppermute | solution.py:17
  103.5 5.9 %collective-permute-done.5.rest_7_ = bf16[4,9,2,16,128]{4,3,2,1,0:T(8,128)(2,1)S(1)} collective-permute-done((bf16[4,9,2,16,128]{4,3,2,1,0:T(8,128)(2,1)S(1)}, bf16[4,9,2,16,128]{4,3,2,1,0:T(8,128)(2,1)S(1)}, u32[]{:S(2)}, u32[]{:S(2)}) %collective-permute-start.5) | collective-permute-done | bytes 294944 | tf_op jit(solution)/shard_map/ppermute | solution.py:17
  110.3 4.4 %all-gather.7.cloned.1.call-done = bf16[32,15,2,16,128]{4,3,2,1,0:T(8,128)(2,1)} async-done(((bf16[4,15,2,16,128]{4,3,2,1,0:T(8,128)(2,1)}), bf16[32,15,2,16,128]{4,3,2,1,0:T(8,128)(2,1)}) %all-gather.7.cloned.1.call-update) | async-done | bytes 3932176 | tf_op jit(solution)/shard_map/all_gather | solution.py:156
  114.7 9.3 %shard_map.83 = (bf16[512,128]{1,0:T(8,128)(2,1)}, bf16[512,128]{1,0:T(8,128)(2,1)}) custom-call(s32[2,64]{1,0:T(2,128)} %get-tuple-element.32.zi_ref, s32[2,64]{1,0:T(2,128)} %get-tuple-element.33.xc_ref, s32[2,64]{1,0:T(2,128)} %get-tuple-element.31.s_ref, f32[16,16]{1,0:T(8,128)} %add.141.c_ref, s32[2,4]{1,0:T(2,128)} %bitcast.50, ...), custom_call_target="tpu_custom_call" | custom-call | flops 1073741824 | bytes 8388608 | tf_op jit(solution)/shard_map/pallas_call | solution.py:195
  128.5 3.4 %collective-permute-start.8 = (bf16[64,16,128]{2,1,0:T(8,128)(2,1)S(1)}, bf16[64,16,128]{2,1,0:T(8,128)(2,1)S(1)}, u32[]{:S(2)}, u32[]{:S(2)}) collective-permute-start(bf16[64,16,128]{2,1,0:T(8,128)(2,1)S(1)} %pad_maximum_fusion.1.refs_0_), channel_id=1, source_target_pairs={{0,64},{64,128},{128,192},{192,256},{256,320},{320,384},{384,448},... | collective-permute-start | bytes 786440 | tf_op jit(solution)/shard_map/ppermute | solution.py:17
  131.9 3.7 %collective-permute-start.9 = (bf16[64,16,128]{2,1,0:T(8,128)(2,1)S(1)}, bf16[64,16,128]{2,1,0:T(8,128)(2,1)S(1)}, u32[]{:S(2)}, u32[]{:S(2)}) collective-permute-start(bf16[64,16,128]{2,1,0:T(8,128)(2,1)S(1)} %pad_maximum_fusion.1.refs_0_), channel_id=1, source_target_pairs={{0,448},{64,0},{128,64},{192,128},{256,192},{320,256},{384,320},{4... | collective-permute-start | bytes 786440 | tf_op jit(solution)/shard_map/ppermute | solution.py:17
  135.6 4.4 %collective-permute-done.8.refs_1_ = bf16[64,16,128]{2,1,0:T(8,128)(2,1)S(1)} collective-permute-done((bf16[64,16,128]{2,1,0:T(8,128)(2,1)S(1)}, bf16[64,16,128]{2,1,0:T(8,128)(2,1)S(1)}, u32[]{:S(2)}, u32[]{:S(2)}) %collective-permute-start.8) | collective-permute-done | bytes 262176 | tf_op jit(solution)/shard_map/ppermute | solution.py:17
  140.0 2.2 %collective-permute-start.10 = (bf16[64,16,128]{2,1,0:T(8,128)(2,1)S(1)}, bf16[64,16,128]{2,1,0:T(8,128)(2,1)S(1)}, u32[]{:S(2)}, u32[]{:S(2)}) collective-permute-start(bf16[64,16,128]{2,1,0:T(8,128)(2,1)S(1)} %collective-permute-done.8.refs_1_), channel_id=1, source_target_pairs={{0,64},{64,128},{128,192},{192,256},{256,320},{320,384},{384,448},... | collective-permute-start | bytes 786440 | tf_op jit(solution)/shard_map/ppermute | solution.py:17
  142.2 4.9 %collective-permute-start.11 = (bf16[64,16,128]{2,1,0:T(8,128)(2,1)S(1)}, bf16[64,16,128]{2,1,0:T(8,128)(2,1)S(1)}, u32[]{:S(2)}, u32[]{:S(2)}) collective-permute-start(bf16[64,16,128]{2,1,0:T(8,128)(2,1)S(1)} %collective-permute-done.9.refs_2_), channel_id=1, source_target_pairs={{0,448},{64,0},{128,64},{192,128},{256,192},{320,256},{384,320},{4... | collective-permute-start | bytes 786440 | tf_op jit(solution)/shard_map/ppermute | solution.py:17
  147.0 3.6 %collective-permute-done.10.refs_3_ = bf16[64,16,128]{2,1,0:T(8,128)(2,1)S(1)} collective-permute-done((bf16[64,16,128]{2,1,0:T(8,128)(2,1)S(1)}, bf16[64,16,128]{2,1,0:T(8,128)(2,1)S(1)}, u32[]{:S(2)}, u32[]{:S(2)}) %collective-permute-start.10) | collective-permute-done | bytes 262176 | tf_op jit(solution)/shard_map/ppermute | solution.py:17
  152.5 5.1 %collective-permute-start.13 = (bf16[64,16,128]{2,1,0:T(8,128)(2,1)S(1)}, bf16[64,16,128]{2,1,0:T(8,128)(2,1)S(1)}, u32[]{:S(2)}, u32[]{:S(2)}) collective-permute-start(bf16[64,16,128]{2,1,0:T(8,128)(2,1)S(1)} %collective-permute-done.11.refs_4_), channel_id=1, source_target_pairs={{0,448},{64,0},{128,64},{192,128},{256,192},{320,256},{384,320},{4... | collective-permute-start | bytes 786440 | tf_op jit(solution)/shard_map/ppermute | solution.py:17
  157.7 2.6 %collective-permute-done.12.refs_5_ = bf16[64,16,128]{2,1,0:T(8,128)(2,1)S(1)} collective-permute-done((bf16[64,16,128]{2,1,0:T(8,128)(2,1)S(1)}, bf16[64,16,128]{2,1,0:T(8,128)(2,1)S(1)}, u32[]{:S(2)}, u32[]{:S(2)}) %collective-permute-start.12) | collective-permute-done | bytes 262176 | tf_op jit(solution)/shard_map/ppermute | solution.py:17
  162.4 7.4 %collective-permute-done.14.refs_7_ = bf16[64,16,128]{2,1,0:T(8,128)(2,1)S(1)} collective-permute-done((bf16[64,16,128]{2,1,0:T(8,128)(2,1)S(1)}, bf16[64,16,128]{2,1,0:T(8,128)(2,1)S(1)}, u32[]{:S(2)}, u32[]{:S(2)}) %collective-permute-start.14) | collective-permute-done | bytes 262176 | tf_op jit(solution)/shard_map/ppermute | solution.py:17
  169.8 3.5 %shard_map.84 = bf16[64,128,128]{2,1,0:T(8,128)(2,1)} custom-call(s32[8]{0:T(128)S(1)} %stack.68.place_ref, bf16[64,16,128]{2,1,0:T(8,128)(2,1)S(1)} %pad_maximum_fusion.1.refs_0_, bf16[64,16,128]{2,1,0:T(8,128)(2,1)S(1)} %collective-permute-done.8.refs_1_, bf16[64,16,128]{2,1,0:T(8,128)(2,1)S(1)} %collective-permute-done.9.refs_2_, ...), custom_call_target="tpu_custom_call" | custom-call | flops 268435456 | bytes 4194304 | tf_op jit(solution)/shard_map/pallas_call | solution.py:217
  (71 shorter events, 26.6 us)
Async XLA Ops:
  6.5 69.2 %all-gather.5.cloned.1.call-start = ((), (), s32[]{:S(2)}) async-start(), calls=%async_computation.3 | async-start | bytes 2359296 | tf_op jit(solution)/shard_map/all_gather | solution.py:147
  9.9 33.3 %copy-start.1 = (bf16[64,128,128]{2,1,0:T(8,128)(2,1)S(1)}, bf16[64,128,128]{2,1,0:T(8,128)(2,1)}, u32[]{:S(2)}) copy-start(bf16[64,128,128]{2,1,0:T(8,128)(2,1)} %th_own.1) | copy-start | bytes 6291460
  28.3 27.8 %copy-start.8 = (s32[64]{0:T(128)S(1)}, s32[64]{0:T(128)}, u32[]{:S(2)}) copy-start(s32[64]{0:T(128)} %param.15) | copy-start | bytes 772
  28.3 27.8 %copy-start.9 = (s32[64,1]{0,1:T(1,128)S(1)}, s32[64,1]{0,1:T(1,128)}, u32[]{:S(2)}) copy-start(s32[64,1]{0,1:T(1,128)} %param.14) | copy-start | bytes 772
  28.3 27.8 %copy-start.10 = (s32[4]{0:T(128)S(1)}, s32[4]{0:T(128)}, u32[]{:S(2)}) copy-start(s32[4]{0:T(128)} %param.12) | copy-start | bytes 52
  29.2 13.1 %all-to-all-start.1 = ((bf16[4,15,2,16,128]{4,3,2,1,0:T(8,128)(2,1)}), bf16[4,15,2,16,128]{4,3,2,1,0:T(8,128)(2,1)S(1)}, u32[]{:S(2)}, u32[]{:S(2)}) async-start(bf16[4,15,2,16,128]{4,3,2,1,0:T(8,128)(2,1)} %broadcast_in_dim.21), calls=%async_computation.1 | async-start | bytes 983040 | tf_op jit(solution)/shard_map/all_to_all | solution.py:154
  34.0 80.7 %all-gather.7.cloned.1.call-start = ((), (), s32[]{:S(2)}) async-start(), calls=%async_computation.4 | async-start | bytes 4423680 | tf_op jit(solution)/shard_map/all_gather | solution.py:156
  43.1 17.3 %collective-permute-start = (bf16[64,128,128]{2,1,0:T(8,128)(2,1)S(1)}, bf16[64,128,128]{2,1,0:T(8,128)(2,1)}, u32[]{:S(2)}, u32[]{:S(2)}) collective-permute-start(bf16[64,128,128]{2,1,0:T(8,128)(2,1)S(1)} %copy-done.1), channel_id=1, source_target_pairs={{0,1},{1,0},{2,3},{3,2},{4,5},{5,4},{6,7},{7,6},{8,9},{9,8},{10,11... | collective-permute-start | bytes 6291464 | tf_op jit(solution)/shard_map/ppermute | solution.py:31
  46.0 29.7 %all-to-all-start.2 = ((bf16[8,9,2,16,128]{4,3,2,1,0:T(8,128)(2,1)}), bf16[8,9,2,16,128]{4,3,2,1,0:T(8,128)(2,1)S(1)}, u32[]{:S(2)}, u32[]{:S(2)}) async-start(bf16[8,9,2,16,128]{4,3,2,1,0:T(8,128)(2,1)} %broadcast_in_dim.22), calls=%async_computation.2 | async-start | bytes 1179648 | tf_op jit(solution)/shard_map/all_to_all | solution.py:158
  56.2 3.0 %collective-permute-start.1 = (s32[2,64]{1,0:T(2,128)S(1)}, s32[2,64]{1,0:T(2,128)S(1)}, u32[]{:S(2)}, u32[]{:S(2)}) collective-permute-start(s32[2,64]{1,0:T(2,128)S(1)} %get-tuple-element.34), channel_id=1, source_target_pairs={{0,1},{1,0},{2,3},{3,2},{4,5},{5,4},{6,7},{7,6},{8,9},{9,8},{10,11... | collective-permute-start | bytes 1544 | tf_op jit(solution)/shard_map/ppermute | solution.py:31
  75.7 39.0 %copy-start.2 = (bf16[8,9,2,16,128]{4,3,2,1,0:T(8,128)(2,1)}, bf16[8,9,2,16,128]{4,3,2,1,0:T(8,128)(2,1)S(1)}, u32[]{:S(2)}) copy-start(bf16[8,9,2,16,128]{4,3,2,1,0:T(8,128)(2,1)S(1)} %all-to-all-done.2.rest_4_) | copy-start | bytes 1769476
  75.7 34.6 %collective-permute-start.2 = (bf16[8,2,4,128,128]{4,3,2,1,0:T(8,128)(2,1)}, bf16[8,2,4,128,128]{4,3,2,1,0:T(8,128)(2,1)S(1)}, u32[]{:S(2)}, u32[]{:S(2)}) collective-permute-start(bf16[8,2,4,128,128]{4,3,2,1,0:T(8,128)(2,1)} %bitcast.42), channel_id=1, source_target_pairs={{0,1},{1,0},{2,3},{3,2},{4,5},{5,4},{6,7},{7,6},{8,9},{9,8},{10,11... | collective-permute-start | bytes 6291464 | tf_op jit(solution)/shard_map/ppermute | solution.py:31
  77.7 31.7 %collective-permute-start.4 = (bf16[8,9,2,16,128]{4,3,2,1,0:T(8,128)(2,1)S(1)}, bf16[8,9,2,16,128]{4,3,2,1,0:T(8,128)(2,1)S(1)}, u32[]{:S(2)}, u32[]{:S(2)}) collective-permute-start(bf16[8,9,2,16,128]{4,3,2,1,0:T(8,128)(2,1)S(1)} %all-to-all-done.2.rest_4_), channel_id=1, source_target_pairs={{0,6},{2,0},{4,2},{6,4},{1,7},{3,1},{5,3},{7,5},{8,14},{10,8},{12,... | collective-permute-start | bytes 1769480 | tf_op jit(solution)/shard_map/ppermute | solution.py:17
  79.6 30.7 %collective-permute-start.3 = (bf16[8,9,2,16,128]{4,3,2,1,0:T(8,128)(2,1)S(1)}, bf16[8,9,2,16,128]{4,3,2,1,0:T(8,128)(2,1)}, u32[]{:S(2)}, u32[]{:S(2)}) collective-permute-start(bf16[8,9,2,16,128]{4,3,2,1,0:T(8,128)(2,1)S(1)} %all-to-all-done.2.rest_4_), channel_id=1, source_target_pairs={{0,2},{2,4},{4,6},{6,0},{1,3},{3,5},{5,7},{7,1},{8,10},{10,12},{12... | collective-permute-start | bytes 1769480 | tf_op jit(solution)/shard_map/ppermute | solution.py:17
  84.9 18.7 %collective-permute-start.6 = (bf16[4,9,2,16,128]{4,3,2,1,0:T(8,128)(2,1)S(1)}, bf16[4,9,2,16,128]{4,3,2,1,0:T(8,128)(2,1)S(1)}, u32[]{:S(2)}, u32[]{:S(2)}) collective-permute-start(bf16[4,9,2,16,128]{4,3,2,1,0:T(8,128)(2,1)S(1)} %get-tuple-element.25), channel_id=1, source_target_pairs={{0,4},{2,6},{4,0},{6,2},{1,5},{3,7},{5,1},{7,3},{8,12},{10,14},{12... | collective-permute-start | bytes 884744 | tf_op jit(solution)/shard_map/ppermute | solution.py:17
  87.7 21.8 %collective-permute-start.5 = (bf16[4,9,2,16,128]{4,3,2,1,0:T(8,128)(2,1)S(1)}, bf16[4,9,2,16,128]{4,3,2,1,0:T(8,128)(2,1)S(1)}, u32[]{:S(2)}, u32[]{:S(2)}) collective-permute-start(bf16[4,9,2,16,128]{4,3,2,1,0:T(8,128)(2,1)S(1)} %get-tuple-element.26), channel_id=1, source_target_pairs={{0,4},{2,6},{4,0},{6,2},{1,5},{3,7},{5,1},{7,3},{8,12},{10,14},{12... | collective-permute-start | bytes 884744 | tf_op jit(solution)/shard_map/ppermute | solution.py:17
  124.1 3.5 %collective-permute-start.7 = (bf16[512,128]{1,0:T(8,128)(2,1)}, bf16[512,128]{1,0:T(8,128)(2,1)S(1)}, u32[]{:S(2)}, u32[]{:S(2)}) collective-permute-start(bf16[512,128]{1,0:T(8,128)(2,1)} %get-tuple-element.24), channel_id=1, source_target_pairs={{0,1},{1,0},{2,3},{3,2},{4,5},{5,4},{6,7},{7,6},{8,9},{9,8},{10,11... | collective-permute-start | bytes 393224 | tf_op jit(solution)/shard_map/ppermute | solution.py:31
  128.5 11.5 %collective-permute-start.8 = (bf16[64,16,128]{2,1,0:T(8,128)(2,1)S(1)}, bf16[64,16,128]{2,1,0:T(8,128)(2,1)S(1)}, u32[]{:S(2)}, u32[]{:S(2)}) collective-permute-start(bf16[64,16,128]{2,1,0:T(8,128)(2,1)S(1)} %pad_maximum_fusion.1.refs_0_), channel_id=1, source_target_pairs={{0,64},{64,128},{128,192},{192,256},{256,320},{320,384},{384,448},... | collective-permute-start | bytes 786440 | tf_op jit(solution)/shard_map/ppermute | solution.py:17
  131.9 10.2 %collective-permute-start.9 = (bf16[64,16,128]{2,1,0:T(8,128)(2,1)S(1)}, bf16[64,16,128]{2,1,0:T(8,128)(2,1)S(1)}, u32[]{:S(2)}, u32[]{:S(2)}) collective-permute-start(bf16[64,16,128]{2,1,0:T(8,128)(2,1)S(1)} %pad_maximum_fusion.1.refs_0_), channel_id=1, source_target_pairs={{0,448},{64,0},{128,64},{192,128},{256,192},{320,256},{384,320},{4... | collective-permute-start | bytes 786440 | tf_op jit(solution)/shard_map/ppermute | solution.py:17
  140.0 10.6 %collective-permute-start.10 = (bf16[64,16,128]{2,1,0:T(8,128)(2,1)S(1)}, bf16[64,16,128]{2,1,0:T(8,128)(2,1)S(1)}, u32[]{:S(2)}, u32[]{:S(2)}) collective-permute-start(bf16[64,16,128]{2,1,0:T(8,128)(2,1)S(1)} %collective-permute-done.8.refs_1_), channel_id=1, source_target_pairs={{0,64},{64,128},{128,192},{192,256},{256,320},{320,384},{384,448},... | collective-permute-start | bytes 786440 | tf_op jit(solution)/shard_map/ppermute | solution.py:17
  142.2 10.3 %collective-permute-start.11 = (bf16[64,16,128]{2,1,0:T(8,128)(2,1)S(1)}, bf16[64,16,128]{2,1,0:T(8,128)(2,1)S(1)}, u32[]{:S(2)}, u32[]{:S(2)}) collective-permute-start(bf16[64,16,128]{2,1,0:T(8,128)(2,1)S(1)} %collective-permute-done.9.refs_2_), channel_id=1, source_target_pairs={{0,448},{64,0},{128,64},{192,128},{256,192},{320,256},{384,320},{4... | collective-permute-start | bytes 786440 | tf_op jit(solution)/shard_map/ppermute | solution.py:17
  150.6 9.7 %collective-permute-start.12 = (bf16[64,16,128]{2,1,0:T(8,128)(2,1)S(1)}, bf16[64,16,128]{2,1,0:T(8,128)(2,1)S(1)}, u32[]{:S(2)}, u32[]{:S(2)}) collective-permute-start(bf16[64,16,128]{2,1,0:T(8,128)(2,1)S(1)} %collective-permute-done.10.refs_3_), channel_id=1, source_target_pairs={{0,64},{64,128},{128,192},{192,256},{256,320},{320,384},{384,448},... | collective-permute-start | bytes 786440 | tf_op jit(solution)/shard_map/ppermute | solution.py:17
  152.5 9.9 %collective-permute-start.13 = (bf16[64,16,128]{2,1,0:T(8,128)(2,1)S(1)}, bf16[64,16,128]{2,1,0:T(8,128)(2,1)S(1)}, u32[]{:S(2)}, u32[]{:S(2)}) collective-permute-start(bf16[64,16,128]{2,1,0:T(8,128)(2,1)S(1)} %collective-permute-done.11.refs_4_), channel_id=1, source_target_pairs={{0,448},{64,0},{128,64},{192,128},{256,192},{320,256},{384,320},{4... | collective-permute-start | bytes 786440 | tf_op jit(solution)/shard_map/ppermute | solution.py:17
  160.3 9.5 %collective-permute-start.14 = (bf16[64,16,128]{2,1,0:T(8,128)(2,1)S(1)}, bf16[64,16,128]{2,1,0:T(8,128)(2,1)S(1)}, u32[]{:S(2)}, u32[]{:S(2)}) collective-permute-start(bf16[64,16,128]{2,1,0:T(8,128)(2,1)S(1)} %collective-permute-done.12.refs_5_), channel_id=1, source_target_pairs={{0,64},{64,128},{128,192},{192,256},{256,320},{320,384},{384,448},... | collective-permute-start | bytes 786440 | tf_op jit(solution)/shard_map/ppermute | solution.py:17
  (6 other events, 20.1 us)
Sparse Core Ops, SparseCore 0:
  9.4 48.0 all-gather.4
  59.6 55.0 all-gather.6

commit v4 on v3

--- a/solution.py
+++ b/solution.py
@@ -18,13 +18,12 @@
 
 
 def both_ways(x, axis):
-    up = down = x
-    pieces, owners = [x], [0]
-    for step in range(1, 4):
-        up, down = shift(up, axis, 1), shift(down, axis, -1)
-        pieces += [up, down]
-        owners += [-step, step]
-    return pieces + [shift(up, axis, 1)], owners + [-4]
+    up, down = shift(x, axis, 1), shift(x, axis, -1)
+    up2, up3 = shift(up, axis, 1), shift(up, axis, 2)
+    down2, down3 = shift(down, axis, -1), shift(down, axis, -2)
+    far = shift(up3, axis, 1)
+    pieces = lax.optimization_barrier([up, down, up2, down2, up3, down3, far])
+    return [x, *pieces], [0, -1, 1, -2, 2, -3, 3, -4]
 
 
 def swap(x):
@@ -212,6 +211,7 @@
     piece = jnp.concatenate(
         [jnp.where(first, mine, other), jnp.where(first, other, mine)], axis=1
     )
+    piece = lax.optimization_barrier(piece)
     pieces, owners = both_ways(piece, "y")
     place = jnp.stack([(at_y + o + 8) % 8 for o in owners]).astype(jnp.int32)
     return pl.pallas_call(

time: 181 us -> 180 us (level)
  transfers between devices with their start and end apart: 19 -> 19, of which waited for: 12 -> 13; matrix products, arithmetic and copies ran while one was open for 4% -> 4% of each run, Pallas kernels for 4% -> 4%
where the time goes in v4:
time: 180 us; the launch traced here: 179 us
  starting transfers between devices  60 us (33%)
  waiting for transfers between devices  56.4 us (31%)
  Pallas kernels  19.2 us (11%)
  blocking collectives  18.3 us (10%)
  between operations  13.9 us (8%)
  local copies, waits for them, and re-layouts  6.2 us (3%)
  other arithmetic  4.7 us (3%)
    ppermute x11, starting transfers between devices, shift(): return lax.ppermute(x, axis, [(i, (i + by) % count) for i in range(count)])  37.1 us
    ppermute x11, waiting for transfers between devices, shift(): return lax.ppermute(x, axis, [(i, (i + by) % count) for i in range(count)])  33.7 us
    all_to_all x1, blocking collectives, on_device(): lax.all_to_all(right, ('y', 'c'), split_axis=0, concat_axis=0, tiled=True)  18.3 us
    all_to_all x1, starting transfers between devices, on_device(): one = lax.all_to_all(one, 'z', split_axis=0, concat_axis=0, tiled=True)  10.1 us
    pallas_call x1, Pallas kernels, on_device(): pl.pallas_call(contract_kernel, out_shape=(jax.ShapeDtypeStruct((512, 128...  9.33 us
    all_to_all x1, waiting for transfers between devices, on_device(): two = lax.all_to_all(two, 'x', split_axis=0, concat_axis=0, tiled=True)  8.3 us
    ppermute x4, starting transfers between devices, swap(): return lax.ppermute(x, 'c', [(0, 1), (1, 0)])  8.01 us
    all_to_all x1, waiting for transfers between devices, on_device(): one = lax.all_to_all(one, 'z', split_axis=0, concat_axis=0, tiled=True)  6.88 us
  transfers between devices with their start and end apart: 19, of which 13 were waited for; matrix products, arithmetic and copies ran while one was open for 4% of the time, Pallas kernels for 4%

profile of v4, /device:TPU:6, one launch (start us, length us, event | category | flops | bytes accessed | tf_op | source)
XLA Modules:
  0.0 178.7 jit_solution(12491766946322633977)
XLA Ops:
  10.0 18.3 %all_to_all.15 = bf16[16,64,128]{2,1,0:T(8,128)(2,1)S(1)} all-to-all(bf16[16,64,128]{2,1,0:T(8,128)(2,1)S(1)} %pad_maximum_fusion), channel_id=1, replica_groups=mesh['y'=8,'z'=8,'x'=4,'c'=2] {'y','c'}, dimensions={0} | all-to-all | bytes 524288 | tf_op jit(solution)/shard_map/all_to_all | solution.py:147
  29.2 4.8 %all-to-all-start.1 = ((bf16[4,15,2,16,128]{4,3,2,1,0:T(8,128)(2,1)}), bf16[4,15,2,16,128]{4,3,2,1,0:T(8,128)(2,1)S(1)}, u32[]{:S(2)}, u32[]{:S(2)}) async-start(bf16[4,15,2,16,128]{4,3,2,1,0:T(8,128)(2,1)} %broadcast_in_dim.21), calls=%async_computation.1 | async-start | bytes 983040 | tf_op jit(solution)/shard_map/all_to_all | solution.py:153
  34.0 8.3 %all-to-all-done.1 = bf16[4,15,2,16,128]{4,3,2,1,0:T(8,128)(2,1)S(1)} async-done(((bf16[4,15,2,16,128]{4,3,2,1,0:T(8,128)(2,1)}), bf16[4,15,2,16,128]{4,3,2,1,0:T(8,128)(2,1)S(1)}, u32[]{:S(2)}, u32[]{:S(2)}) %all-to-all-start.1) | async-done | bytes 491552 | tf_op jit(solution)/shard_map/all_to_all | solution.py:153
  46.0 10.1 %all-to-all-start.2 = ((bf16[8,9,2,16,128]{4,3,2,1,0:T(8,128)(2,1)}), bf16[8,9,2,16,128]{4,3,2,1,0:T(8,128)(2,1)S(1)}, u32[]{:S(2)}, u32[]{:S(2)}) async-start(bf16[8,9,2,16,128]{4,3,2,1,0:T(8,128)(2,1)} %broadcast_in_dim.22), calls=%async_computation.2 | async-start | bytes 1179648 | tf_op jit(solution)/shard_map/all_to_all | solution.py:157
  60.5 6.4 %shard_map.82.rest_0_ = bf16[2,64,128,128]{3,2,1,0:T(8,128)(2,1)S(1)} custom-call(bf16[64,128,128]{2,1,0:T(8,128)(2,1)S(1)} %copy-done.1, bf16[64,128,128]{2,1,0:T(8,128)(2,1)} %collective-permute-done.th_sib), custom_call_target="tpu_custom_call" | custom-call | flops 536870912 | bytes 8388608 | tf_op jit(solution)/shard_map/pallas_call | solution.py:173
  68.9 6.9 %all-to-all-done.2.rest_4_ = bf16[8,9,2,16,128]{4,3,2,1,0:T(8,128)(2,1)S(1)} async-done(((bf16[8,9,2,16,128]{4,3,2,1,0:T(8,128)(2,1)}), bf16[8,9,2,16,128]{4,3,2,1,0:T(8,128)(2,1)S(1)}, u32[]{:S(2)}, u32[]{:S(2)}) %all-to-all-start.2) | async-done | bytes 589856 | tf_op jit(solution)/shard_map/all_to_all | solution.py:157
  79.6 5.1 %collective-permute-start.3 = (bf16[8,9,2,16,128]{4,3,2,1,0:T(8,128)(2,1)S(1)}, bf16[8,9,2,16,128]{4,3,2,1,0:T(8,128)(2,1)}, u32[]{:S(2)}, u32[]{:S(2)}) collective-permute-start(bf16[8,9,2,16,128]{4,3,2,1,0:T(8,128)(2,1)S(1)} %all-to-all-done.2.rest_4_), channel_id=1, source_target_pairs={{0,2},{2,4},{4,6},{6,0},{1,3},{3,5},{5,7},{7,1},{8,10},{10,12},{12... | collective-permute-start | bytes 1769480 | tf_op jit(solution)/shard_map/ppermute | solution.py:17
  84.9 2.8 %collective-permute-start.6 = (bf16[4,9,2,16,128]{4,3,2,1,0:T(8,128)(2,1)S(1)}, bf16[4,9,2,16,128]{4,3,2,1,0:T(8,128)(2,1)S(1)}, u32[]{:S(2)}, u32[]{:S(2)}) collective-permute-start(bf16[4,9,2,16,128]{4,3,2,1,0:T(8,128)(2,1)S(1)} %get-tuple-element.39), channel_id=1, source_target_pairs={{0,4},{2,6},{4,0},{6,2},{1,5},{3,7},{5,1},{7,3},{8,12},{10,14},{12... | collective-permute-start | bytes 884744 | tf_op jit(solution)/shard_map/ppermute | solution.py:17
  87.7 4.6 %collective-permute-start.5 = (bf16[4,9,2,16,128]{4,3,2,1,0:T(8,128)(2,1)S(1)}, bf16[4,9,2,16,128]{4,3,2,1,0:T(8,128)(2,1)S(1)}, u32[]{:S(2)}, u32[]{:S(2)}) collective-permute-start(bf16[4,9,2,16,128]{4,3,2,1,0:T(8,128)(2,1)S(1)} %get-tuple-element.40), channel_id=1, source_target_pairs={{0,4},{2,6},{4,0},{6,2},{1,5},{3,7},{5,1},{7,3},{8,12},{10,14},{12... | collective-permute-start | bytes 884744 | tf_op jit(solution)/shard_map/ppermute | solution.py:17
  93.5 10.0 %collective-permute-done.6.rest_8_ = bf16[4,9,2,16,128]{4,3,2,1,0:T(8,128)(2,1)S(1)} collective-permute-done((bf16[4,9,2,16,128]{4,3,2,1,0:T(8,128)(2,1)S(1)}, bf16[4,9,2,16,128]{4,3,2,1,0:T(8,128)(2,1)S(1)}, u32[]{:S(2)}, u32[]{:S(2)}) %collective-permute-start.6) | collective-permute-done | bytes 294944 | tf_op jit(solution)/shard_map/ppermute | solution.py:17
  103.5 5.9 %collective-permute-done.5.rest_7_ = bf16[4,9,2,16,128]{4,3,2,1,0:T(8,128)(2,1)S(1)} collective-permute-done((bf16[4,9,2,16,128]{4,3,2,1,0:T(8,128)(2,1)S(1)}, bf16[4,9,2,16,128]{4,3,2,1,0:T(8,128)(2,1)S(1)}, u32[]{:S(2)}, u32[]{:S(2)}) %collective-permute-start.5) | collective-permute-done | bytes 294944 | tf_op jit(solution)/shard_map/ppermute | solution.py:17
  110.3 4.4 %all-gather.7.cloned.1.call-done = bf16[32,15,2,16,128]{4,3,2,1,0:T(8,128)(2,1)} async-done(((bf16[4,15,2,16,128]{4,3,2,1,0:T(8,128)(2,1)}), bf16[32,15,2,16,128]{4,3,2,1,0:T(8,128)(2,1)}) %all-gather.7.cloned.1.call-update) | async-done | bytes 3932176 | tf_op jit(solution)/shard_map/all_gather | solution.py:155
  114.7 9.3 %shard_map.83 = (bf16[512,128]{1,0:T(8,128)(2,1)}, bf16[512,128]{1,0:T(8,128)(2,1)}) custom-call(s32[2,64]{1,0:T(2,128)} %get-tuple-element.46.zi_ref, s32[2,64]{1,0:T(2,128)} %get-tuple-element.47.xc_ref, s32[2,64]{1,0:T(2,128)} %get-tuple-element.45.s_ref, f32[16,16]{1,0:T(8,128)} %add.141.c_ref, s32[2,4]{1,0:T(2,128)} %bitcast.50, ...), custom_call_target="tpu_custom_call" | custom-call | flops 1073741824 | bytes 8388608 | tf_op jit(solution)/shard_map/pallas_call | solution.py:194
  128.5 3.4 %collective-permute-start.8 = (bf16[64,16,128]{2,1,0:T(8,128)(2,1)S(1)}, bf16[64,16,128]{2,1,0:T(8,128)(2,1)S(1)}, u32[]{:S(2)}, u32[]{:S(2)}) collective-permute-start(bf16[64,16,128]{2,1,0:T(8,128)(2,1)S(1)} %pad_maximum_fusion.1.refs_0_), channel_id=1, source_target_pairs={{0,64},{64,128},{128,192},{192,256},{256,320},{320,384},{384,448},... | collective-permute-start | bytes 786440 | tf_op jit(solution)/shard_map/ppermute | solution.py:17
  131.9 3.7 %collective-permute-start.9 = (bf16[64,16,128]{2,1,0:T(8,128)(2,1)S(1)}, bf16[64,16,128]{2,1,0:T(8,128)(2,1)S(1)}, u32[]{:S(2)}, u32[]{:S(2)}) collective-permute-start(bf16[64,16,128]{2,1,0:T(8,128)(2,1)S(1)} %pad_maximum_fusion.1.refs_0_), channel_id=1, source_target_pairs={{0,448},{64,0},{128,64},{192,128},{256,192},{320,256},{384,320},{4... | collective-permute-start | bytes 786440 | tf_op jit(solution)/shard_map/ppermute | solution.py:17
  135.6 4.4 %collective-permute-done.8.refs_1_ = bf16[64,16,128]{2,1,0:T(8,128)(2,1)S(1)} collective-permute-done((bf16[64,16,128]{2,1,0:T(8,128)(2,1)S(1)}, bf16[64,16,128]{2,1,0:T(8,128)(2,1)S(1)}, u32[]{:S(2)}, u32[]{:S(2)}) %collective-permute-start.8) | collective-permute-done | bytes 262176 | tf_op jit(solution)/shard_map/ppermute | solution.py:17
  139.9 3.1 %collective-permute-start.12 = (bf16[64,16,128]{2,1,0:T(8,128)(2,1)S(1)}, bf16[64,16,128]{2,1,0:T(8,128)(2,1)S(1)}, u32[]{:S(2)}, u32[]{:S(2)}) collective-permute-start(bf16[64,16,128]{2,1,0:T(8,128)(2,1)S(1)} %collective-permute-done.8.refs_1_), channel_id=1, source_target_pairs={{0,128},{64,192},{128,256},{192,320},{256,384},{320,448},{384,0},{... | collective-permute-start | bytes 786440 | tf_op jit(solution)/shard_map/ppermute | solution.py:17
  143.1 4.8 %collective-permute-start.13 = (bf16[64,16,128]{2,1,0:T(8,128)(2,1)S(1)}, bf16[64,16,128]{2,1,0:T(8,128)(2,1)S(1)}, u32[]{:S(2)}, u32[]{:S(2)}) collective-permute-start(bf16[64,16,128]{2,1,0:T(8,128)(2,1)S(1)} %collective-permute-done.9.refs_2_), channel_id=1, source_target_pairs={{0,384},{64,448},{128,0},{192,64},{256,128},{320,192},{384,256},{4... | collective-permute-start | bytes 786440 | tf_op jit(solution)/shard_map/ppermute | solution.py:17
  147.9 2.3 %collective-permute-start.11 = (bf16[64,16,128]{2,1,0:T(8,128)(2,1)S(1)}, bf16[64,16,128]{2,1,0:T(8,128)(2,1)S(1)}, u32[]{:S(2)}, u32[]{:S(2)}) collective-permute-start(bf16[64,16,128]{2,1,0:T(8,128)(2,1)S(1)} %collective-permute-done.9.refs_2_), channel_id=1, source_target_pairs={{0,448},{64,0},{128,64},{192,128},{256,192},{320,256},{384,320},{4... | collective-permute-start | bytes 786440 | tf_op jit(solution)/shard_map/ppermute | solution.py:17
  150.2 3.5 %collective-permute-start.10 = (bf16[64,16,128]{2,1,0:T(8,128)(2,1)S(1)}, bf16[64,16,128]{2,1,0:T(8,128)(2,1)S(1)}, u32[]{:S(2)}, u32[]{:S(2)}) collective-permute-start(bf16[64,16,128]{2,1,0:T(8,128)(2,1)S(1)} %collective-permute-done.8.refs_1_), channel_id=1, source_target_pairs={{0,64},{64,128},{128,192},{192,256},{256,320},{320,384},{384,448},... | collective-permute-start | bytes 786440 | tf_op jit(solution)/shard_map/ppermute | solution.py:17
  153.8 3.4 %collective-permute-done.12.refs_5_ = bf16[64,16,128]{2,1,0:T(8,128)(2,1)S(1)} collective-permute-done((bf16[64,16,128]{2,1,0:T(8,128)(2,1)S(1)}, bf16[64,16,128]{2,1,0:T(8,128)(2,1)S(1)}, u32[]{:S(2)}, u32[]{:S(2)}) %collective-permute-start.12) | collective-permute-done | bytes 262176 | tf_op jit(solution)/shard_map/ppermute | solution.py:17
  160.4 4.3 %collective-permute-done.11.refs_4_ = bf16[64,16,128]{2,1,0:T(8,128)(2,1)S(1)} collective-permute-done((bf16[64,16,128]{2,1,0:T(8,128)(2,1)S(1)}, bf16[64,16,128]{2,1,0:T(8,128)(2,1)S(1)}, u32[]{:S(2)}, u32[]{:S(2)}) %collective-permute-start.11) | collective-permute-done | bytes 262176 | tf_op jit(solution)/shard_map/ppermute | solution.py:17
  164.7 3.7 %collective-permute-done.14.refs_7_ = bf16[64,16,128]{2,1,0:T(8,128)(2,1)S(1)} collective-permute-done((bf16[64,16,128]{2,1,0:T(8,128)(2,1)S(1)}, bf16[64,16,128]{2,1,0:T(8,128)(2,1)S(1)}, u32[]{:S(2)}, u32[]{:S(2)}) %collective-permute-start.14) | collective-permute-done | bytes 262176 | tf_op jit(solution)/shard_map/ppermute | solution.py:17
  168.4 3.5 %shard_map.84 = bf16[64,128,128]{2,1,0:T(8,128)(2,1)} custom-call(s32[8]{0:T(128)S(1)} %stack.68.place_ref, bf16[64,16,128]{2,1,0:T(8,128)(2,1)S(1)} %pad_maximum_fusion.1.refs_0_, bf16[64,16,128]{2,1,0:T(8,128)(2,1)S(1)} %collective-permute-done.8.refs_1_, bf16[64,16,128]{2,1,0:T(8,128)(2,1)S(1)} %collective-permute-done.9.refs_2_, ...), custom_call_target="tpu_custom_call" | custom-call | flops 268435456 | bytes 4194304 | tf_op jit(solution)/shard_map/pallas_call | solution.py:217
  (71 shorter events, 28.0 us)
Async XLA Ops:
  6.5 69.2 %all-gather.5.cloned.1.call-start = ((), (), s32[]{:S(2)}) async-start(), calls=%async_computation.3 | async-start | bytes 2359296 | tf_op jit(solution)/shard_map/all_gather | solution.py:146
  9.9 33.3 %copy-start.1 = (bf16[64,128,128]{2,1,0:T(8,128)(2,1)S(1)}, bf16[64,128,128]{2,1,0:T(8,128)(2,1)}, u32[]{:S(2)}) copy-start(bf16[64,128,128]{2,1,0:T(8,128)(2,1)} %th_own.1) | copy-start | bytes 6291460
  28.3 27.8 %copy-start.8 = (s32[64]{0:T(128)S(1)}, s32[64]{0:T(128)}, u32[]{:S(2)}) copy-start(s32[64]{0:T(128)} %param.15) | copy-start | bytes 772
  28.3 27.8 %copy-start.9 = (s32[64,1]{0,1:T(1,128)S(1)}, s32[64,1]{0,1:T(1,128)}, u32[]{:S(2)}) copy-start(s32[64,1]{0,1:T(1,128)} %param.14) | copy-start | bytes 772
  28.3 27.8 %copy-start.10 = (s32[4]{0:T(128)S(1)}, s32[4]{0:T(128)}, u32[]{:S(2)}) copy-start(s32[4]{0:T(128)} %param.12) | copy-start | bytes 52
  29.2 13.1 %all-to-all-start.1 = ((bf16[4,15,2,16,128]{4,3,2,1,0:T(8,128)(2,1)}), bf16[4,15,2,16,128]{4,3,2,1,0:T(8,128)(2,1)S(1)}, u32[]{:S(2)}, u32[]{:S(2)}) async-start(bf16[4,15,2,16,128]{4,3,2,1,0:T(8,128)(2,1)} %broadcast_in_dim.21), calls=%async_computation.1 | async-start | bytes 983040 | tf_op jit(solution)/shard_map/all_to_all | solution.py:153
  34.0 80.7 %all-gather.7.cloned.1.call-start = ((), (), s32[]{:S(2)}) async-start(), calls=%async_computation.4 | async-start | bytes 4423680 | tf_op jit(solution)/shard_map/all_gather | solution.py:155
  43.1 17.3 %collective-permute-start = (bf16[64,128,128]{2,1,0:T(8,128)(2,1)S(1)}, bf16[64,128,128]{2,1,0:T(8,128)(2,1)}, u32[]{:S(2)}, u32[]{:S(2)}) collective-permute-start(bf16[64,128,128]{2,1,0:T(8,128)(2,1)S(1)} %copy-done.1), channel_id=1, source_target_pairs={{0,1},{1,0},{2,3},{3,2},{4,5},{5,4},{6,7},{7,6},{8,9},{9,8},{10,11... | collective-permute-start | bytes 6291464 | tf_op jit(solution)/shard_map/ppermute | solution.py:30
  46.0 29.7 %all-to-all-start.2 = ((bf16[8,9,2,16,128]{4,3,2,1,0:T(8,128)(2,1)}), bf16[8,9,2,16,128]{4,3,2,1,0:T(8,128)(2,1)S(1)}, u32[]{:S(2)}, u32[]{:S(2)}) async-start(bf16[8,9,2,16,128]{4,3,2,1,0:T(8,128)(2,1)} %broadcast_in_dim.22), calls=%async_computation.2 | async-start | bytes 1179648 | tf_op jit(solution)/shard_map/all_to_all | solution.py:157
  56.2 3.0 %collective-permute-start.1 = (s32[2,64]{1,0:T(2,128)S(1)}, s32[2,64]{1,0:T(2,128)S(1)}, u32[]{:S(2)}, u32[]{:S(2)}) collective-permute-start(s32[2,64]{1,0:T(2,128)S(1)} %get-tuple-element.48), channel_id=1, source_target_pairs={{0,1},{1,0},{2,3},{3,2},{4,5},{5,4},{6,7},{7,6},{8,9},{9,8},{10,11... | collective-permute-start | bytes 1544 | tf_op jit(solution)/shard_map/ppermute | solution.py:30
  75.7 39.0 %copy-start.2 = (bf16[8,9,2,16,128]{4,3,2,1,0:T(8,128)(2,1)}, bf16[8,9,2,16,128]{4,3,2,1,0:T(8,128)(2,1)S(1)}, u32[]{:S(2)}) copy-start(bf16[8,9,2,16,128]{4,3,2,1,0:T(8,128)(2,1)S(1)} %all-to-all-done.2.rest_4_) | copy-start | bytes 1769476
  75.7 34.6 %collective-permute-start.2 = (bf16[8,2,4,128,128]{4,3,2,1,0:T(8,128)(2,1)}, bf16[8,2,4,128,128]{4,3,2,1,0:T(8,128)(2,1)S(1)}, u32[]{:S(2)}, u32[]{:S(2)}) collective-permute-start(bf16[8,2,4,128,128]{4,3,2,1,0:T(8,128)(2,1)} %bitcast.42), channel_id=1, source_target_pairs={{0,1},{1,0},{2,3},{3,2},{4,5},{5,4},{6,7},{7,6},{8,9},{9,8},{10,11... | collective-permute-start | bytes 6291464 | tf_op jit(solution)/shard_map/ppermute | solution.py:30
  77.7 31.7 %collective-permute-start.4 = (bf16[8,9,2,16,128]{4,3,2,1,0:T(8,128)(2,1)S(1)}, bf16[8,9,2,16,128]{4,3,2,1,0:T(8,128)(2,1)S(1)}, u32[]{:S(2)}, u32[]{:S(2)}) collective-permute-start(bf16[8,9,2,16,128]{4,3,2,1,0:T(8,128)(2,1)S(1)} %all-to-all-done.2.rest_4_), channel_id=1, source_target_pairs={{0,6},{2,0},{4,2},{6,4},{1,7},{3,1},{5,3},{7,5},{8,14},{10,8},{12,... | collective-permute-start | bytes 1769480 | tf_op jit(solution)/shard_map/ppermute | solution.py:17
  79.6 30.7 %collective-permute-start.3 = (bf16[8,9,2,16,128]{4,3,2,1,0:T(8,128)(2,1)S(1)}, bf16[8,9,2,16,128]{4,3,2,1,0:T(8,128)(2,1)}, u32[]{:S(2)}, u32[]{:S(2)}) collective-permute-start(bf16[8,9,2,16,128]{4,3,2,1,0:T(8,128)(2,1)S(1)} %all-to-all-done.2.rest_4_), channel_id=1, source_target_pairs={{0,2},{2,4},{4,6},{6,0},{1,3},{3,5},{5,7},{7,1},{8,10},{10,12},{12... | collective-permute-start | bytes 1769480 | tf_op jit(solution)/shard_map/ppermute | solution.py:17
  84.9 18.7 %collective-permute-start.6 = (bf16[4,9,2,16,128]{4,3,2,1,0:T(8,128)(2,1)S(1)}, bf16[4,9,2,16,128]{4,3,2,1,0:T(8,128)(2,1)S(1)}, u32[]{:S(2)}, u32[]{:S(2)}) collective-permute-start(bf16[4,9,2,16,128]{4,3,2,1,0:T(8,128)(2,1)S(1)} %get-tuple-element.39), channel_id=1, source_target_pairs={{0,4},{2,6},{4,0},{6,2},{1,5},{3,7},{5,1},{7,3},{8,12},{10,14},{12... | collective-permute-start | bytes 884744 | tf_op jit(solution)/shard_map/ppermute | solution.py:17
  87.7 21.8 %collective-permute-start.5 = (bf16[4,9,2,16,128]{4,3,2,1,0:T(8,128)(2,1)S(1)}, bf16[4,9,2,16,128]{4,3,2,1,0:T(8,128)(2,1)S(1)}, u32[]{:S(2)}, u32[]{:S(2)}) collective-permute-start(bf16[4,9,2,16,128]{4,3,2,1,0:T(8,128)(2,1)S(1)} %get-tuple-element.40), channel_id=1, source_target_pairs={{0,4},{2,6},{4,0},{6,2},{1,5},{3,7},{5,1},{7,3},{8,12},{10,14},{12... | collective-permute-start | bytes 884744 | tf_op jit(solution)/shard_map/ppermute | solution.py:17
  124.0 3.5 %collective-permute-start.7 = (bf16[512,128]{1,0:T(8,128)(2,1)}, bf16[512,128]{1,0:T(8,128)(2,1)S(1)}, u32[]{:S(2)}, u32[]{:S(2)}) collective-permute-start(bf16[512,128]{1,0:T(8,128)(2,1)} %get-tuple-element.31), channel_id=1, source_target_pairs={{0,1},{1,0},{2,3},{3,2},{4,5},{5,4},{6,7},{7,6},{8,9},{9,8},{10,11... | collective-permute-start | bytes 393224 | tf_op jit(solution)/shard_map/ppermute | solution.py:30
  128.5 11.5 %collective-permute-start.8 = (bf16[64,16,128]{2,1,0:T(8,128)(2,1)S(1)}, bf16[64,16,128]{2,1,0:T(8,128)(2,1)S(1)}, u32[]{:S(2)}, u32[]{:S(2)}) collective-permute-start(bf16[64,16,128]{2,1,0:T(8,128)(2,1)S(1)} %pad_maximum_fusion.1.refs_0_), channel_id=1, source_target_pairs={{0,64},{64,128},{128,192},{192,256},{256,320},{320,384},{384,448},... | collective-permute-start | bytes 786440 | tf_op jit(solution)/shard_map/ppermute | solution.py:17
  131.9 11.2 %collective-permute-start.9 = (bf16[64,16,128]{2,1,0:T(8,128)(2,1)S(1)}, bf16[64,16,128]{2,1,0:T(8,128)(2,1)S(1)}, u32[]{:S(2)}, u32[]{:S(2)}) collective-permute-start(bf16[64,16,128]{2,1,0:T(8,128)(2,1)S(1)} %pad_maximum_fusion.1.refs_0_), channel_id=1, source_target_pairs={{0,448},{64,0},{128,64},{192,128},{256,192},{320,256},{384,320},{4... | collective-permute-start | bytes 786440 | tf_op jit(solution)/shard_map/ppermute | solution.py:17
  139.9 17.2 %collective-permute-start.12 = (bf16[64,16,128]{2,1,0:T(8,128)(2,1)S(1)}, bf16[64,16,128]{2,1,0:T(8,128)(2,1)S(1)}, u32[]{:S(2)}, u32[]{:S(2)}) collective-permute-start(bf16[64,16,128]{2,1,0:T(8,128)(2,1)S(1)} %collective-permute-done.8.refs_1_), channel_id=1, source_target_pairs={{0,128},{64,192},{128,256},{192,320},{256,384},{320,448},{384,0},{... | collective-permute-start | bytes 786440 | tf_op jit(solution)/shard_map/ppermute | solution.py:17
  143.1 17.3 %collective-permute-start.13 = (bf16[64,16,128]{2,1,0:T(8,128)(2,1)S(1)}, bf16[64,16,128]{2,1,0:T(8,128)(2,1)S(1)}, u32[]{:S(2)}, u32[]{:S(2)}) collective-permute-start(bf16[64,16,128]{2,1,0:T(8,128)(2,1)S(1)} %collective-permute-done.9.refs_2_), channel_id=1, source_target_pairs={{0,384},{64,448},{128,0},{192,64},{256,128},{320,192},{384,256},{4... | collective-permute-start | bytes 786440 | tf_op jit(solution)/shard_map/ppermute | solution.py:17
  147.9 16.7 %collective-permute-start.11 = (bf16[64,16,128]{2,1,0:T(8,128)(2,1)S(1)}, bf16[64,16,128]{2,1,0:T(8,128)(2,1)S(1)}, u32[]{:S(2)}, u32[]{:S(2)}) collective-permute-start(bf16[64,16,128]{2,1,0:T(8,128)(2,1)S(1)} %collective-permute-done.9.refs_2_), channel_id=1, source_target_pairs={{0,448},{64,0},{128,64},{192,128},{256,192},{320,256},{384,320},{4... | collective-permute-start | bytes 786440 | tf_op jit(solution)/shard_map/ppermute | solution.py:17
  150.2 14.4 %collective-permute-start.10 = (bf16[64,16,128]{2,1,0:T(8,128)(2,1)S(1)}, bf16[64,16,128]{2,1,0:T(8,128)(2,1)S(1)}, u32[]{:S(2)}, u32[]{:S(2)}) collective-permute-start(bf16[64,16,128]{2,1,0:T(8,128)(2,1)S(1)} %collective-permute-done.8.refs_1_), channel_id=1, source_target_pairs={{0,64},{64,128},{128,192},{192,256},{256,320},{320,384},{384,448},... | collective-permute-start | bytes 786440 | tf_op jit(solution)/shard_map/ppermute | solution.py:17
  157.1 11.2 %collective-permute-start.14 = (bf16[64,16,128]{2,1,0:T(8,128)(2,1)S(1)}, bf16[64,16,128]{2,1,0:T(8,128)(2,1)S(1)}, u32[]{:S(2)}, u32[]{:S(2)}) collective-permute-start(bf16[64,16,128]{2,1,0:T(8,128)(2,1)S(1)} %collective-permute-done.12.refs_5_), channel_id=1, source_target_pairs={{0,64},{64,128},{128,192},{192,256},{256,320},{320,384},{384,448},... | collective-permute-start | bytes 786440 | tf_op jit(solution)/shard_map/ppermute | solution.py:17
  (6 other events, 20.1 us)
Sparse Core Ops, SparseCore 0:
  9.4 48.0 all-gather.4
  59.6 55.0 all-gather.6
